TPU v7x, 256 devices: a whole 4x4x8 slice. The times are simulated.
256 devices in a mesh: examples: 32 (over y, z), shard: 4 (over x), reps: 2 (over core).
Axes of the slice: x: 4, y: 4, z: 8, core: 2. Of those that a mesh axis runs over, the one named last changes fastest.
Arguments:
- train_inputs: bfloat16 [4096, 8, 4096], P(('examples', 'reps')), may hold values from -10 to 10
- train_grads: bfloat16 [4096, 8, 14336], P(('examples', 'reps'), None, 'shard'), may hold values from -10 to 10
- query_inputs: bfloat16 [128, 8, 4096], P(('examples', 'reps')), may hold values from -10 to 10
- query_grads: bfloat16 [128, 8, 14336], P(('examples', 'reps'), None, 'shard'), may hold values from -10 to 10
- block_maps: bfloat16 [128, 32, 16], replicated, may hold values from -0.125 to 0.125
- block_index: int32 [128], replicated, may hold values from 0 to 1
- block_sign: int32 [128], replicated, may hold values from 0 to 1
- ff_map: bfloat16 [14336, 16], P('shard'), may hold values from -0.09375 to 0.09375
Outputs:
- scores: float32 [4096, 128], P(('examples', 'reps'))
All inputs are finite; a program needn't handle non-finite values.
Results may differ from a plain program's by a relative error of at most 0.0003.
Values sent between devices are 32-bit elements; how exact they have to be, the bound alone decides.
No kernel may reach another device: no remote copies, remote signals or barrier semaphores. Data moves between devices by JAX's collectives and lax.ppermute only.
A program may use at most 64 MiB of HBM per device.

v0:
```python
import math

import jax
import jax.numpy as jnp
from jax import lax
from jax.sharding import PartitionSpec as P

D = 4096
OUTB = 2
K1 = 32
K2 = 16
KB = 512
RANK = 8


ridge_weight = 1.0


def partner_2(block, axis, stride):
    count = lax.axis_size(axis)
    route = []
    for low in range(count):
        high = low | 1 << stride
        if high != low and high < count:
            route += [(low, high), (high, low)]
    return lax.ppermute(block, axis, route)


def build_map(block_maps, block_index, block_sign):
    chooser = (block_index[:, None] == jnp.arange(OUTB, dtype=jnp.int32)[None, :]).astype(
        jnp.float32
    )
    chooser = chooser * (2 * block_sign - 1).astype(jnp.float32)[:, None]
    dense = block_maps.astype(jnp.float32)[:, :, None, :] * chooser[:, None, :, None]
    return dense.reshape(D, K1).astype(jnp.bfloat16)


def features(inputs, grad_rows, input_map, ff_part):
    row_count = inputs.shape[0]
    left_part = jnp.dot(
        inputs.reshape(row_count * RANK, D), input_map, preferred_element_type=jnp.float32
    )
    right_part = jnp.dot(
        grad_rows.reshape(row_count * RANK, grad_rows.shape[2]),
        ff_part,
        preferred_element_type=jnp.float32,
    )
    outer = jnp.einsum(
        "erk,erl->ekl",
        left_part.reshape(row_count, RANK, K1),
        right_part.reshape(row_count, RANK, K2),
        precision=lax.Precision.HIGHEST,
    )
    return outer.reshape(row_count, K1 * K2) / math.sqrt(RANK)


def on_device(
    train_inputs,
    train_grads,
    query_inputs,
    query_grads,
    block_maps,
    block_index,
    block_sign,
    ff_map,
):
    input_map = build_map(block_maps, block_index, block_sign)
    train_feats = features(train_inputs, train_grads, input_map, ff_map)
    query_feats = features(query_inputs, query_grads, input_map, ff_map)
    example_count = lax.axis_size("examples")
    rep_count = lax.axis_size("reps")
    shard_count = lax.axis_size("shard")
    leaves = example_count * rep_count
    examples_all = train_feats.shape[0] * leaves
    identity = jnp.eye(KB, dtype=jnp.float32)
    local_gram = (
        jnp.dot(train_feats.T, train_feats, precision=lax.Precision.HIGHEST) / examples_all
        + ridge_weight / leaves * identity
    )
    gram_total = local_gram
    for section_bit in range(example_count.bit_length() - 1):
        partner = partner_2(gram_total, "examples", section_bit)
        gram_total = gram_total + partner
    partner = partner_2(gram_total, "reps", 0)
    gram_total = gram_total + partner
    lower_factor = jnp.linalg.cholesky(gram_total)
    all_queries = lax.all_gather(query_feats, ("examples", "reps"), axis=0, tiled=True)
    solved = jax.scipy.linalg.cho_solve((lower_factor, True), all_queries.T)
    partial_value = jnp.dot(train_feats, solved, precision=lax.Precision.HIGHEST)
    summed = lax.psum(partial_value, "shard")
    return summed / math.sqrt(KB * shard_count)


def solution(mesh):
    placed = (
        P(("examples", "reps"), None, None),
        P(("examples", "reps"), None, "shard"),
        P(("examples", "reps"), None, None),
        P(("examples", "reps"), None, "shard"),
        P(),
        P(),
        P(),
        P("shard", None),
    )
    return jax.shard_map(
        on_device,
        mesh=mesh,
        in_specs=placed,
        out_specs=P(("examples", "reps"), None),
        check_vma=False,
    )
```

profile of v0, /device:TPU:8, one launch (start us, length us, event | category | flops | bytes accessed | tf_op | source)
XLA Modules:
  0.0 400.3 jit_solution(12035643959372580231)
XLA Ops:
  4.1 3.5 fusion.3
  7.8 3.1 fusion.47
  13.3 2.0 collective-permute-start
  15.3 23.2 %collective-permute-done = f32[512,512]{0,1:T(8,128)S(1)} collective-permute-done((f32[512,512]{0,1:T(8,128)S(1)}, f32[512,512]{0,1:T(8,128)S(1)}, u32[]{:S(2)}, u32[]{:S(2)}) %collective-permute-start) | collective-permute-done | bytes 1048608 | tf_op jit(solution)/shard_map/ppermute | solution.py:26
  38.6 3.4 collective-permute-start.1
  42.0 44.9 %collective-permute-done.1 = f32[512,512]{0,1:T(8,128)S(1)} collective-permute-done((f32[512,512]{0,1:T(8,128)S(1)}, f32[512,512]{0,1:T(8,128)S(1)}, u32[]{:S(2)}, u32[]{:S(2)}) %collective-permute-start.1) | collective-permute-done | bytes 1048608 | tf_op jit(solution)/shard_map/ppermute | solution.py:26
  87.2 6.3 %collective-permute-start.2 = (f32[512,512]{0,1:T(8,128)S(1)}, f32[512,512]{0,1:T(8,128)S(1)}, u32[]{:S(2)}, u32[]{:S(2)}) collective-permute-start(f32[512,512]{0,1:T(8,128)S(1)} %add.70), channel_id=1, source_target_pairs={{0,32},{32,0},{8,40},{40,8},{16,48},{48,16},{24,56},{56,24},{64,96... | collective-permute-start | bytes 3145736 | tf_op jit(solution)/shard_map/ppermute | solution.py:26
  93.4 45.8 %collective-permute-done.2 = f32[512,512]{0,1:T(8,128)S(1)} collective-permute-done((f32[512,512]{0,1:T(8,128)S(1)}, f32[512,512]{0,1:T(8,128)S(1)}, u32[]{:S(2)}, u32[]{:S(2)}) %collective-permute-start.2) | collective-permute-done | bytes 1048608 | tf_op jit(solution)/shard_map/ppermute | solution.py:26
  140.0 23.5 %collective-permute-done.3 = f32[512,512]{0,1:T(8,128)S(1)} collective-permute-done((f32[512,512]{0,1:T(8,128)S(1)}, f32[512,512]{0,1:T(8,128)S(1)}, u32[]{:S(2)}, u32[]{:S(2)}) %collective-permute-start.3) | collective-permute-done | bytes 1048608 | tf_op jit(solution)/shard_map/ppermute | solution.py:26
  163.6 2.4 collective-permute-start.4
  166.0 22.2 %collective-permute-done.4 = f32[512,512]{0,1:T(8,128)S(1)} collective-permute-done((f32[512,512]{0,1:T(8,128)S(1)}, f32[512,512]{0,1:T(8,128)S(1)}, u32[]{:S(2)}, u32[]{:S(2)}) %collective-permute-start.4) | collective-permute-done | bytes 1048608 | tf_op jit(solution)/shard_map/ppermute | solution.py:26
  189.3 46.0 %all-gather = f32[64,2,512]{2,1,0:T(2,128)S(1)} all-gather(f32[1,2,512]{2,1,0:T(2,128)S(1)} %reshape.155), channel_id=1, replica_groups=mesh['examples'=32,'shard'=4,'reps'=2] {'examples','reps'}, dimensions={0}, use_global_device_ids=true | all-gather | bytes 266240 | tf_op jit(solution)/shard_map/all_gather | solution.py:87
  236.3 1.4 add.74
  238.4 11.7 %cholesky.103 = f32[128,128]{1,0:T(8,128)S(1)} custom-call(f32[128,128]{1,0:T(8,128)S(1)} %cholesky.263), custom_call_target="Cholesky" | custom-call | tf_op jit(solution)/shard_map/jit(cholesky)/cholesky | solution.py:86
  250.2 9.8 %custom-call.34 = f32[1,128,128]{1,2,0:T(8,128)S(1)} custom-call(f32[1,128,128]{2,1,0:T(8,128)S(1)} %get-tuple-element.44), custom_call_target="InvertDiagBlocksLowerTriangular" | custom-call | tf_op jit(solution)/shard_map/jit(cholesky)/cholesky | solution.py:86
  260.8 11.9 %cholesky.215 = f32[128,128]{1,0:T(8,128)S(1)} custom-call(f32[128,128]{1,0:T(8,128)S(1)} %cholesky.267), custom_call_target="Cholesky" | custom-call | tf_op jit(solution)/shard_map/jit(cholesky)/cholesky | solution.py:86
  272.9 9.8 %custom-call.35 = f32[1,128,128]{1,2,0:T(8,128)S(1)} custom-call(f32[1,128,128]{2,1,0:T(8,128)S(1)} %get-tuple-element.42), custom_call_target="InvertDiagBlocksLowerTriangular" | custom-call | tf_op jit(solution)/shard_map/jit(cholesky)/cholesky | solution.py:86
  283.8 11.7 %cholesky.236 = f32[128,128]{1,0:T(8,128)S(1)} custom-call(f32[128,128]{1,0:T(8,128)S(1)} %cholesky.272), custom_call_target="Cholesky" | custom-call | tf_op jit(solution)/shard_map/jit(cholesky)/cholesky | solution.py:86
  295.6 9.8 %custom-call.36 = f32[1,128,128]{1,2,0:T(8,128)S(1)} custom-call(f32[1,128,128]{2,1,0:T(8,128)S(1)} %get-tuple-element.40), custom_call_target="InvertDiagBlocksLowerTriangular" | custom-call | tf_op jit(solution)/shard_map/jit(cholesky)/cholesky | solution.py:86
  306.3 12.0 %cholesky.253 = f32[128,128]{1,0:T(8,128)S(1)} custom-call(f32[128,128]{1,0:T(8,128)S(1)} %slice_subtract_fusion.2), custom_call_target="Cholesky" | custom-call | tf_op jit(solution)/shard_map/jit(cholesky)/cholesky | solution.py:86
  323.1 11.0 %while.1 = (s32[]{:T(128)}, f32[512,512]{0,1:T(8,128)S(1)}, s32[4,2]{0,1:T(2,128)S(1)}, f32[4,128,128]{2,1,0:T(8,128)}, s32[]{:T(128)}) while((s32[]{:T(128)}, f32[512,512]{0,1:T(8,128)S(1)}, s32[4,2]{0,1:T(2,128)S(1)}, f32[4,128,128]{2,1,0:T(8,128)}, s32[]{:T(128)}) %tuple.27), condition=%wide.while_cond, body=%wide.while_body.sunk | while | flops 2 | bytes 393329 | solution.py:88
  323.8 1.3 dynamic-slice.7
  334.1 40.1 %custom-call.37 = f32[4,128,128]{1,2,0:T(8,128)S(1)} custom-call(f32[4,128,128]{2,1,0:T(8,128)} %get-tuple-element.12), custom_call_target="InvertDiagBlocksLowerTriangular" | custom-call | tf_op jit(solution)/shard_map/jit(_cho_solve)/triangular_solve | solution.py:88
  382.2 17.1 %psum.7 = f32[64,128]{1,0:T(8,128)S(1)} all-reduce(f32[64,128]{1,0:T(8,128)S(1)} %fusion.9), channel_id=1, replica_groups=mesh['examples'=32,'shard'=4,'reps'=2] {'shard'}, use_global_device_ids=true, to_apply=%region_8.9 | all-reduce | flops 8192 | bytes 65536 | tf_op jit(solution)/shard_map/psum | solution.py:90
  (97 shorter events, 33.9 us)
Async XLA Ops:
  0.0 188.5 %copy-start = (bf16[2,8,4096]{2,1,0:T(8,128)(2,1)S(1)}, bf16[2,8,4096]{2,1,0:T(8,128)(2,1)}, u32[]{:S(2)}) copy-start(bf16[2,8,4096]{2,1,0:T(8,128)(2,1)} %param.10) | copy-start | bytes 393220
  2.6 5.1 %copy-start.1 = (bf16[3584,16]{0,1:T(8,128)(2,1)S(1)}, bf16[3584,16]{0,1:T(8,128)(2,1)}, u32[]{:S(2)}) copy-start(bf16[3584,16]{0,1:T(8,128)(2,1)} %param.15) | copy-start | bytes 344068
  13.3 25.2 %collective-permute-start = (f32[512,512]{0,1:T(8,128)S(1)}, f32[512,512]{0,1:T(8,128)S(1)}, u32[]{:S(2)}, u32[]{:S(2)}) collective-permute-start(f32[512,512]{0,1:T(8,128)S(1)} %fusion.2), channel_id=1, source_target_pairs={{0,8},{8,0},{16,24},{24,16},{32,40},{40,32},{48,56},{56,48},{64,72... | collective-permute-start | bytes 3145736 | tf_op jit(solution)/shard_map/ppermute | solution.py:26
  38.6 48.3 %collective-permute-start.1 = (f32[512,512]{0,1:T(8,128)S(1)}, f32[512,512]{0,1:T(8,128)S(1)}, u32[]{:S(2)}, u32[]{:S(2)}) collective-permute-start(f32[512,512]{0,1:T(8,128)S(1)} %add.69), channel_id=1, source_target_pairs={{0,16},{16,0},{8,24},{24,8},{32,48},{48,32},{40,56},{56,40},{64,80... | collective-permute-start | bytes 3145736 | tf_op jit(solution)/shard_map/ppermute | solution.py:26
  87.2 52.0 %collective-permute-start.2 = (f32[512,512]{0,1:T(8,128)S(1)}, f32[512,512]{0,1:T(8,128)S(1)}, u32[]{:S(2)}, u32[]{:S(2)}) collective-permute-start(f32[512,512]{0,1:T(8,128)S(1)} %add.70), channel_id=1, source_target_pairs={{0,32},{32,0},{8,40},{40,8},{16,48},{48,16},{24,56},{56,24},{64,96... | collective-permute-start | bytes 3145736 | tf_op jit(solution)/shard_map/ppermute | solution.py:26
  139.4 49.3 %copy-start.2 = (bf16[2,8,3584]{2,1,0:T(8,128)(2,1)S(1)}, bf16[2,8,3584]{2,1,0:T(8,128)(2,1)}, u32[]{:S(2)}) copy-start(bf16[2,8,3584]{2,1,0:T(8,128)(2,1)} %param.11) | copy-start | bytes 344068
  139.4 24.0 %collective-permute-start.3 = (f32[512,512]{0,1:T(8,128)S(1)}, f32[512,512]{0,1:T(8,128)S(1)}, u32[]{:S(2)}, u32[]{:S(2)}) collective-permute-start(f32[512,512]{0,1:T(8,128)S(1)} %add.71), channel_id=1, source_target_pairs={{0,64},{64,0},{8,72},{72,8},{16,80},{80,16},{24,88},{88,24},{32,96... | collective-permute-start | bytes 3145736 | tf_op jit(solution)/shard_map/ppermute | solution.py:26
  163.6 24.6 %collective-permute-start.4 = (f32[512,512]{0,1:T(8,128)S(1)}, f32[512,512]{0,1:T(8,128)S(1)}, u32[]{:S(2)}, u32[]{:S(2)}) collective-permute-start(f32[512,512]{0,1:T(8,128)S(1)} %add.72), channel_id=1, source_target_pairs={{0,128},{128,0},{8,136},{136,8},{16,144},{144,16},{24,152},{152,24... | collective-permute-start | bytes 3145736 | tf_op jit(solution)/shard_map/ppermute | solution.py:26
  188.4 47.9 %collective-permute-start.5 = (f32[512,512]{0,1:T(8,128)S(1)}, f32[512,512]{0,1:T(8,128)}, u32[]{:S(2)}, u32[]{:S(2)}) collective-permute-start(f32[512,512]{0,1:T(8,128)S(1)} %add.73), channel_id=1, source_target_pairs={{0,1},{1,0},{2,3},{3,2},{4,5},{5,4},{6,7},{7,6},{8,9},{9,8},{10,11... | collective-permute-start | bytes 3145736 | tf_op jit(solution)/shard_map/ppermute | solution.py:26
where the time goes:
time: 408 us; the launch traced here: 400 us
  waiting for transfers between devices  160 us (39%)
  other arithmetic  124 us (30%)
  blocking collectives  63.1 us (15%)
  matrix products  19.5 us (5%)
  local copies, waits for them, and re-layouts  15.9 us (4%)
  starting transfers between devices  14.6 us (4%)
    ppermute x6, waiting for transfers between devices, partner_2(): return lax.ppermute(block, axis, route)  160 us
    another operation x14, other arithmetic, on_device(): lower_factor = jnp.linalg.cholesky(gram_total)  78.9 us
    all_gather x1, blocking collectives, on_device(): lax.all_gather(query_feats, ('examples', 'reps'), axis=0, tiled=True)  46 us
    another operation x3, other arithmetic, on_device(): solved = jax.scipy.linalg.cho_solve((lower_factor, True), all_queries.T)  40.3 us
    psum x1, blocking collectives, on_device(): summed = lax.psum(partial_value, 'shard')  17.1 us
    ppermute x6, starting transfers between devices, partner_2(): return lax.ppermute(block, axis, route)  14.6 us
    another operation x20, local copies, waits for them, and re-layouts  10.9 us
  transfers between devices with their start and end apart: 6, of which 5 were waited for; matrix products, arithmetic and copies ran while one was open for 0% of the time, Pallas kernels for 0%

commit v1 on v0

v1 whole, which is shorter than its diff:
```python
import math

import jax
import jax.numpy as jnp
from jax import lax
from jax.experimental import pallas as pl
from jax.experimental.pallas import tpu as pltpu
from jax.sharding import PartitionSpec as P

D = 4096
OUTB = 2
K1 = 32
K2 = 16
KB = 512
RANK = 8
EXAMPLES = 4096
RIDGE = 1.0
TILE = 128
PANEL = 16
NB = KB // TILE
PAIRS = [(i, j) for i in range(NB) for j in range(i, NB)]
HALF = len(PAIRS) // 2
NY = 4
NZ = 8
CHUNK = HALF * TILE // NY
HIGH = lax.Precision.HIGHEST
VMEM_LIMIT = 48 << 20


def dot(a, b, contract=(1, 0)):
    return lax.dot_general(
        a,
        b,
        (((contract[0],), (contract[1],)), ((), ())),
        precision=HIGH,
        preferred_element_type=jnp.float32,
    )


def move(block, axis, target):
    count = lax.axis_size(axis)
    return lax.ppermute(block, axis, [(i, target(i)) for i in range(count)])


def along_y(block, step):
    return move(block, "examples", lambda e: (e // NZ + step) % NY * NZ + e % NZ)


def along_z(block, step):
    return move(block, "examples", lambda e: e // NZ * NZ + (e % NZ + step) % NZ)


def build_map(block_maps, block_index, block_sign):
    chooser = (block_index[:, None] == jnp.arange(OUTB, dtype=jnp.int32)[None, :]).astype(
        jnp.float32
    )
    chooser = chooser * (2 * block_sign - 1).astype(jnp.float32)[:, None]
    dense = block_maps.astype(jnp.float32)[:, :, None, :] * chooser[:, None, :, None]
    return dense.reshape(D, K1).astype(jnp.bfloat16)


def features(inputs, grad_rows, input_map, ff_part):
    row_count = inputs.shape[0]
    left_part = jnp.dot(
        inputs.reshape(row_count * RANK, D), input_map, preferred_element_type=jnp.float32
    )
    right_part = jnp.dot(
        grad_rows.reshape(row_count * RANK, grad_rows.shape[2]),
        ff_part,
        preferred_element_type=jnp.float32,
    )
    outer = jnp.einsum(
        "erk,erl->ekl",
        left_part.reshape(row_count, RANK, K1),
        right_part.reshape(row_count, RANK, K2),
        precision=HIGH,
    )
    return outer.reshape(row_count, K1 * K2) / math.sqrt(RANK)


def lookup(table, index):
    value = jnp.int32(table[0])
    for place, entry in enumerate(table[1:], 1):
        value = jnp.where(index == place, jnp.int32(entry), value)
    return value


def gram_kernel(own_ref, other_ref, keep_ref, first_ref, second_ref, third_ref, half):
    rep = lax.axis_index("reps")
    y = lax.axis_index("examples") // NZ
    for place in range(HALF):
        low, high = PAIRS[place], PAIRS[HALF + place]
        row = pl.multiple_of(jnp.where(rep == 0, low[0], high[0]) * TILE, TILE)
        col = pl.multiple_of(jnp.where(rep == 0, low[1], high[1]) * TILE, TILE)
        total = dot(own_ref[:, pl.ds(row, TILE)], own_ref[:, pl.ds(col, TILE)], (0, 0))
        total += dot(other_ref[:, pl.ds(row, TILE)], other_ref[:, pl.ds(col, TILE)], (0, 0))
        half[place * TILE : (place + 1) * TILE, :] = total * (1.0 / EXAMPLES)
    for step, out_ref in enumerate((keep_ref, first_ref, second_ref, third_ref)):
        start = pl.multiple_of(lax.rem(y + step, NY) * CHUNK, 8)
        out_ref[...] = half[pl.ds(start, CHUNK), :]


def panel_inverse(rows, first):
    lane = lax.broadcasted_iota(jnp.int32, (PANEL, TILE), 1)
    row = lax.broadcasted_iota(jnp.int32, (PANEL, TILE), 0)
    spread = [
        jnp.broadcast_to(rows[:, first + j : first + j + 1], (PANEL, TILE)) for j in range(PANEL)
    ]
    inside = (lane >= first) & (lane < first + PANEL)
    rows = jnp.where(inside, (lane - first == row).astype(jnp.float32), rows)
    for j in range(PANEL):
        scale = 1.0 / spread[j][j : j + 1, :]
        pivot_row = rows[j : j + 1, :] * scale
        rows = jnp.where(row == j, pivot_row, rows - spread[j] * pivot_row)
        for k in range(j + 1, PANEL):
            part = spread[k][j : j + 1, :] * scale
            spread[k] = jnp.where(row == j, part, spread[k] - spread[j] * part)
    return rows


def block_inverse(block):
    lane = lax.broadcasted_iota(jnp.int32, (TILE, TILE), 1)
    for first in range(0, TILE, PANEL):
        last = first + PANEL
        fresh = panel_inverse(block[first:last], first)
        update = dot(block[:, first:last], fresh)
        block = jnp.where((lane >= first) & (lane < last), 0.0, block) - update
        parts = [block[:first]] if first else []
        parts.append(fresh)
        if last < TILE:
            parts.append(block[last:])
        block = jnp.concatenate(parts, 0)
    return block


def solve_kernel(own_ref, other_ref, feats_ref, out_ref, gram, query):
    rep = lax.axis_index("reps")
    spot = lax.axis_index("examples")
    y, z = spot // NZ, lax.rem(spot, NZ)
    piece = own_ref.shape[0] // NY
    query_rows = piece - CHUNK
    for side, ref in enumerate((own_ref, other_ref)):
        holder = rep if side == 0 else 1 - rep
        for step in range(NY):
            source = lax.rem(y + NY - step, NY)
            start = pl.multiple_of(holder * (HALF * TILE) + source * CHUNK, 8)
            gram[pl.ds(start, CHUNK), :] = ref[step * piece : step * piece + CHUNK, :]
            at = (side * NY + step) * query_rows
            query[at : at + query_rows, :] = ref[step * piece + CHUNK : (step + 1) * piece, :]

    total_rows = 2 * NY * query_rows
    r = lax.broadcasted_iota(jnp.int32, (total_rows, TILE), 0)
    n = lax.broadcasted_iota(jnp.int32, (total_rows, TILE), 1)
    side, step = r >> 8, (r >> 6) & 3
    group, pair, item, part = (r >> 4) & 3, (r >> 3) & 1, (r >> 2) & 1, r & 3
    shift = jnp.where(group == 0, 0, jnp.where(group == 1, 6, jnp.where(group == 2, 2, 4)))
    source_z = ((z + shift) & 7) ^ pair
    source_y = (y + 4 - step) & 3
    source = (((source_y * NZ + source_z) * 2 + (side ^ rep)) * 2) + item
    values = query[...]
    right = [
        dot(values, ((source == n) & (part == c)).astype(jnp.float32), (0, 0)) for c in range(NB)
    ]

    eye = (
        lax.broadcasted_iota(jnp.int32, (TILE, TILE), 0)
        == lax.broadcasted_iota(jnp.int32, (TILE, TILE), 1)
    ).astype(jnp.float32) * RIDGE
    block = {}
    for place, (i, j) in enumerate(PAIRS):
        value = gram[place * TILE : (place + 1) * TILE, :]
        block[i, j] = value + eye if i == j else value

    solved = []
    for b in range(NB):
        inverse = block_inverse(block[b, b])
        wide = jnp.concatenate([block[b, j] for j in range(b + 1, NB)] + [right[b]], 1)
        done = dot(inverse, wide)
        solved.append(done)
        for i in range(b + 1, NB):
            change = dot(block[b, i], done[:, (i - b - 1) * TILE :], (0, 0))
            for j in range(i, NB):
                block[i, j] = block[i, j] - change[:, (j - i) * TILE : (j - i + 1) * TILE]
            right[i] = right[i] - change[:, (NB - i) * TILE :]
    answer = [None] * NB
    for b in reversed(range(NB)):
        value = solved[b][:, (NB - 1 - b) * TILE :]
        if b < NB - 1:
            later = jnp.concatenate(answer[b + 1 :], 0)
            value = value - dot(solved[b][:, : (NB - 1 - b) * TILE], later)
        answer[b] = value
    out_ref[...] = dot(feats_ref[...], jnp.concatenate(answer, 0)) * (1.0 / math.sqrt(4 * KB))


def on_device(
    train_inputs,
    train_grads,
    query_inputs,
    query_grads,
    block_maps,
    block_index,
    block_sign,
    ff_map,
):
    input_map = build_map(block_maps, block_index, block_sign)
    train_feats = features(train_inputs, train_grads, input_map, ff_map)
    query_feats = features(query_inputs, query_grads, input_map, ff_map)
    other_feats = move(train_feats, "reps", lambda r: 1 - r)
    params = pltpu.CompilerParams(vmem_limit_bytes=VMEM_LIMIT)
    piece = jax.ShapeDtypeStruct((CHUNK, TILE), jnp.float32)
    keep, first, second, third = pl.pallas_call(
        gram_kernel,
        out_shape=[piece] * NY,
        scratch_shapes=[pltpu.VMEM((HALF * TILE, TILE), jnp.float32)],
        compiler_params=params,
    )(train_feats, other_feats)
    second = along_y(second, 2)
    first = along_y(first, 1)
    third = along_y(third, 3)
    gram = keep + first + second + third
    held = jnp.concatenate([gram, query_feats.reshape(-1, TILE)], 0)
    near = move(held, "examples", lambda e: e ^ 1)
    held = jnp.concatenate([gram + near[:CHUNK], held[CHUNK:], near[CHUNK:]], 0)
    far = along_z(held, 4)
    left = along_z(held, 2)
    right = along_z(held, 6)
    gram = held[:CHUNK] + left[:CHUNK] + right[:CHUNK] + far[:CHUNK]
    held = jnp.concatenate([gram, held[CHUNK:], left[CHUNK:], right[CHUNK:], far[CHUNK:]], 0)
    second = along_y(held, 2)
    first = along_y(held, 1)
    third = along_y(held, 3)
    mine = jnp.concatenate([held, first, second, third], 0)
    theirs = move(mine, "reps", lambda r: 1 - r)
    value = pl.pallas_call(
        solve_kernel,
        out_shape=jax.ShapeDtypeStruct((train_feats.shape[0], TILE), jnp.float32),
        scratch_shapes=[
            pltpu.VMEM((len(PAIRS) * TILE, TILE), jnp.float32),
            pltpu.VMEM((KB, TILE), jnp.float32),
        ],
        compiler_params=params,
    )(mine, theirs, train_feats)
    second = move(value, "shard", lambda s: s ^ 2)
    first = move(value, "shard", lambda s: s ^ 1)
    third = move(value, "shard", lambda s: s ^ 3)
    return (value + first) + (second + third)


def solution(mesh):
    placed = (
        P(("examples", "reps"), None, None),
        P(("examples", "reps"), None, "shard"),
        P(("examples", "reps"), None, None),
        P(("examples", "reps"), None, "shard"),
        P(),
        P(),
        P(),
        P("shard", None),
    )
    return jax.shard_map(
        on_device,
        mesh=mesh,
        in_specs=placed,
        out_specs=P(("examples", "reps"), None),
        check_vma=False,
    )
```

time: 408 us -> 84.4 us (0.21)
  the two profiles are of different devices: /device:TPU:8 before, /device:TPU:32 now
where the time goes in v1:
time: 84.4 us; the launch traced here: 84.2 us
  starting transfers between devices  27.3 us (32%)
  waiting for transfers between devices  22.8 us (27%)
  Pallas kernels  20.1 us (24%)
  matrix products  8.28 us (10%)
  local copies, waits for them, and re-layouts  3.16 us (4%)
  other arithmetic  2.33 us (3%)
    ppermute x15, starting transfers between devices, move(): return lax.ppermute(block, axis, [(i, target(i)) for i in range(count)])  27.3 us
    ppermute x15, waiting for transfers between devices, move(): return lax.ppermute(block, axis, [(i, target(i)) for i in range(count)])  22.8 us
    pallas_call x1, Pallas kernels, on_device(): pl.pallas_call(solve_kernel, out_shape=jax.ShapeDtypeStruct((train_feats....  19.3 us
    dot_general x2, matrix products, features(): jnp.dot(inputs.reshape(row_count * RANK, D), input_map, preferred_element...  3.74 us
    dot_general x2, matrix products, features(): jnp.dot(grad_rows.reshape(row_count * RANK, grad_rows.shape[2]), ff_part,...  3.27 us
  transfers between devices with their start and end apart: 15, of which 12 were waited for; matrix products, arithmetic and copies ran while one was open for 1% of the time, Pallas kernels for 0%

profile of v1, /device:TPU:32, one launch (start us, length us, event | category | flops | bytes accessed | tf_op | source)
XLA Modules:
  0.0 84.2 jit_solution(16143910035259907927)
XLA Ops:
  0.0 1.3 %copy.13 = f32[128,32,16]{1,0,2:T(8,128)S(1)} copy(bf16[128,32,16]{0,2,1:T(8,128)(2,1)} %param.12) | data formatting | bytes 393216 | tf_op jit(solution)/shard_map/convert_element_type | solution.py:58
  2.9 1.1 %convert_element_type.26 = bf16[4096,32]{0,1:T(8,128)(2,1)S(1)} reshape(bf16[128,32,2,16]{1,0,3,2:T(8,128)(2,1)S(1)} %multiply_convert_fusion) | data formatting | bytes 524288 | tf_op jit(solution)/shard_map/convert_element_type | solution.py:59
  4.1 3.5 %fusion.2 = f32[512,32]{0,1:T(8,128)S(1)} fusion(bf16[4096,32]{0,1:T(8,128)(2,1)S(1)} %convert_element_type.26, bf16[64,8,4096]{2,1,0:T(8,128)(2,1)} %param.8), kind=kOutput, calls=%fused_computation.4 | convolution fusion | flops 134217728 | bytes 4521984 | tf_op jit(solution)/shard_map/dot_general | solution.py:64
  7.8 3.1 %fusion.9 = f32[64,8,16]{2,1,0:T(8,128)S(1)} fusion(bf16[64,8,3584]{2,1,0:T(8,128)(2,1)} %param.9, bf16[3584,16]{0,1:T(8,128)(2,1)S(1)} %copy-done.1), kind=kOutput, calls=%fused_computation.11 | convolution fusion | flops 58720256 | bytes 3817472 | tf_op jit(solution)/shard_map/dot_general | solution.py:67
  10.9 1.1 %convolution_multiply_fusion = f32[64,32,16]{1,2,0:T(8,128)S(1)} fusion(f32[64,8,16]{2,1,0:T(8,128)S(1)} %fusion.9, f32[512,32]{1,0:T(8,128)S(1)} %copy.14), kind=kOutput, calls=%fused_computation.3 | convolution fusion | flops 3178496 | bytes 229376 | tf_op jit(solution)/shard_map/erk,erl->ekl/dot_general | solution.py:72
  14.6 1.7 %collective-permute-start.1 = (f32[160,128]{1,0:T(8,128)S(1)}, f32[160,128]{1,0:T(8,128)S(1)}, u32[]{:S(2)}, u32[]{:S(2)}) collective-permute-start(f32[160,128]{1,0:T(8,128)S(1)} %get-tuple-element.10), channel_id=1, source_target_pairs={{0,64},{8,72},{16,80},{24,88},{32,96},{40,104},{48,112},{56,120},{... | collective-permute-start | bytes 245768 | tf_op jit(solution)/shard_map/ppermute | solution.py:42
  16.2 2.9 %collective-permute-start.2 = (f32[160,128]{1,0:T(8,128)S(1)}, f32[160,128]{1,0:T(8,128)S(1)}, u32[]{:S(2)}, u32[]{:S(2)}) collective-permute-start(f32[160,128]{1,0:T(8,128)S(1)} %get-tuple-element.11), channel_id=1, source_target_pairs={{0,128},{8,136},{16,144},{24,152},{32,160},{40,168},{48,176},{56,1... | collective-permute-start | bytes 245768 | tf_op jit(solution)/shard_map/ppermute | solution.py:42
  19.1 1.3 %collective-permute-start.3 = (f32[160,128]{1,0:T(8,128)S(1)}, f32[160,128]{1,0:T(8,128)S(1)}, u32[]{:S(2)}, u32[]{:S(2)}) collective-permute-start(f32[160,128]{1,0:T(8,128)S(1)} %get-tuple-element.12), channel_id=1, source_target_pairs={{0,192},{8,200},{16,208},{24,216},{32,224},{40,232},{48,240},{56,2... | collective-permute-start | bytes 245768 | tf_op jit(solution)/shard_map/ppermute | solution.py:42
  20.9 2.5 %collective-permute-done.2 = f32[160,128]{1,0:T(8,128)S(1)} collective-permute-done((f32[160,128]{1,0:T(8,128)S(1)}, f32[160,128]{1,0:T(8,128)S(1)}, u32[]{:S(2)}, u32[]{:S(2)}) %collective-permute-start.2) | collective-permute-done | bytes 81952 | tf_op jit(solution)/shard_map/ppermute | solution.py:42
  24.7 3.5 %collective-permute-done.4 = f32[168,128]{1,0:T(8,128)S(1)} collective-permute-done((f32[168,128]{1,0:T(8,128)S(1)}, f32[168,128]{1,0:T(8,128)S(1)}, u32[]{:S(2)}, u32[]{:S(2)}) %collective-permute-start.4) | collective-permute-done | bytes 86048 | tf_op jit(solution)/shard_map/ppermute | solution.py:42
  28.2 3.3 %collective-permute-start.5 = (f32[176,128]{1,0:T(8,128)S(1)}, f32[176,128]{1,0:T(8,128)S(1)}, u32[]{:S(2)}, u32[]{:S(2)}) collective-permute-start(f32[176,128]{1,0:T(8,128)S(1)} %pad_maximum_fusion), channel_id=1, source_target_pairs={{0,16},{8,24},{16,32},{24,40},{32,48},{40,56},{48,0},{56,8},{64,80... | collective-permute-start | bytes 270344 | tf_op jit(solution)/shard_map/ppermute | solution.py:42
  31.6 2.3 %collective-permute-start.6 = (f32[176,128]{1,0:T(8,128)S(1)}, f32[176,128]{1,0:T(8,128)S(1)}, u32[]{:S(2)}, u32[]{:S(2)}) collective-permute-start(f32[176,128]{1,0:T(8,128)S(1)} %pad_maximum_fusion), channel_id=1, source_target_pairs={{0,48},{8,56},{16,0},{24,8},{32,16},{40,24},{48,32},{56,40},{64,11... | collective-permute-start | bytes 270344 | tf_op jit(solution)/shard_map/ppermute | solution.py:42
  33.9 4.9 %collective-permute-start.7 = (f32[176,128]{1,0:T(8,128)S(1)}, f32[176,128]{1,0:T(8,128)S(1)}, u32[]{:S(2)}, u32[]{:S(2)}) collective-permute-start(f32[176,128]{1,0:T(8,128)S(1)} %pad_maximum_fusion), channel_id=1, source_target_pairs={{0,32},{8,40},{16,48},{24,56},{32,0},{40,8},{48,16},{56,24},{64,96... | collective-permute-start | bytes 270344 | tf_op jit(solution)/shard_map/ppermute | solution.py:42
  38.7 1.1 %collective-permute-done.6 = f32[176,128]{1,0:T(8,128)S(1)} collective-permute-done((f32[176,128]{1,0:T(8,128)S(1)}, f32[176,128]{1,0:T(8,128)S(1)}, u32[]{:S(2)}, u32[]{:S(2)}) %collective-permute-start.6) | collective-permute-done | bytes 90144 | tf_op jit(solution)/shard_map/ppermute | solution.py:42
  39.9 4.3 %collective-permute-done.7 = f32[176,128]{1,0:T(8,128)S(1)} collective-permute-done((f32[176,128]{1,0:T(8,128)S(1)}, f32[176,128]{1,0:T(8,128)S(1)}, u32[]{:S(2)}, u32[]{:S(2)}) %collective-permute-start.7) | collective-permute-done | bytes 90144 | tf_op jit(solution)/shard_map/ppermute | solution.py:42
  45.1 3.0 %collective-permute-start.9 = (f32[224,128]{1,0:T(8,128)S(1)}, f32[224,128]{1,0:T(8,128)S(1)}, u32[]{:S(2)}, u32[]{:S(2)}) collective-permute-start(f32[224,128]{1,0:T(8,128)S(1)} %get-tuple-element.15), channel_id=1, source_target_pairs={{0,128},{8,136},{16,144},{24,152},{32,160},{40,168},{48,176},{56,1... | collective-permute-start | bytes 344072 | tf_op jit(solution)/shard_map/ppermute | solution.py:42
  49.2 1.2 %collective-permute-done.8 = f32[224,128]{1,0:T(8,128)S(1)} collective-permute-done((f32[224,128]{1,0:T(8,128)S(1)}, f32[224,128]{1,0:T(8,128)S(1)}, u32[]{:S(2)}, u32[]{:S(2)}) %collective-permute-start.8) | collective-permute-done | bytes 114720 | tf_op jit(solution)/shard_map/ppermute | solution.py:42
  50.3 1.8 %collective-permute-done.9 = f32[224,128]{1,0:T(8,128)S(1)} collective-permute-done((f32[224,128]{1,0:T(8,128)S(1)}, f32[224,128]{1,0:T(8,128)S(1)}, u32[]{:S(2)}, u32[]{:S(2)}) %collective-permute-start.9) | collective-permute-done | bytes 114720 | tf_op jit(solution)/shard_map/ppermute | solution.py:42
  53.0 1.8 %collective-permute-done.11.other_ref = f32[896,128]{1,0:T(8,128)S(1)} collective-permute-done((f32[896,128]{1,0:T(8,128)S(1)}, f32[896,128]{1,0:T(8,128)S(1)}, u32[]{:S(2)}, u32[]{:S(2)}) %collective-permute-start.11) | collective-permute-done | bytes 458784 | tf_op jit(solution)/shard_map/ppermute | solution.py:42
  54.8 19.3 %shard_map.83 = f32[64,128]{1,0:T(8,128)S(1)} custom-call(f32[896,128]{1,0:T(8,128)S(1)} %constant_dynamic-update-slice_fusion.6.own_ref, f32[896,128]{1,0:T(8,128)S(1)} %collective-permute-done.11.other_ref, f32[64,512]{1,0:T(8,128)S(1)} %copy.17.own_ref.feats_ref), custom_call_target="tpu_custom_call" | custom-call | tf_op jit(solution)/shard_map/pallas_call | solution.py:234
  74.2 1.6 %collective-permute-start.12 = (f32[64,128]{1,0:T(8,128)S(1)}, f32[64,128]{1,0:T(8,128)S(1)}, u32[]{:S(2)}, u32[]{:S(2)}) collective-permute-start(f32[64,128]{1,0:T(8,128)S(1)} %shard_map.83), channel_id=1, source_target_pairs={{0,2},{2,0},{4,6},{6,4},{1,3},{3,1},{5,7},{7,5},{8,10},{10,8},{12,... | collective-permute-start | bytes 98312 | tf_op jit(solution)/shard_map/ppermute | solution.py:42
  75.7 2.7 %collective-permute-start.13 = (f32[64,128]{1,0:T(8,128)S(1)}, f32[64,128]{1,0:T(8,128)S(1)}, u32[]{:S(2)}, u32[]{:S(2)}) collective-permute-start(f32[64,128]{1,0:T(8,128)S(1)} %shard_map.83), channel_id=1, source_target_pairs={{0,4},{2,6},{4,0},{6,2},{1,5},{3,7},{5,1},{7,3},{8,12},{10,14},{12... | collective-permute-start | bytes 98312 | tf_op jit(solution)/shard_map/ppermute | solution.py:42
  78.9 2.2 %collective-permute-done.13 = f32[64,128]{1,0:T(8,128)S(1)} collective-permute-done((f32[64,128]{1,0:T(8,128)S(1)}, f32[64,128]{1,0:T(8,128)S(1)}, u32[]{:S(2)}, u32[]{:S(2)}) %collective-permute-start.13) | collective-permute-done | bytes 32800 | tf_op jit(solution)/shard_map/ppermute | solution.py:42
  81.2 2.4 %collective-permute-done.14 = f32[64,128]{1,0:T(8,128)S(1)} collective-permute-done((f32[64,128]{1,0:T(8,128)S(1)}, f32[64,128]{1,0:T(8,128)S(1)}, u32[]{:S(2)}, u32[]{:S(2)}) %collective-permute-start.14) | collective-permute-done | bytes 32800 | tf_op jit(solution)/shard_map/ppermute | solution.py:42
  (46 shorter events, 10.0 us)
Async XLA Ops:
  0.0 12.6 %copy-start = (bf16[2,8,4096]{2,1,0:T(8,128)(2,1)S(1)}, bf16[2,8,4096]{2,1,0:T(8,128)(2,1)}, u32[]{:S(2)}) copy-start(bf16[2,8,4096]{2,1,0:T(8,128)(2,1)} %param.10) | copy-start | bytes 393220
  2.6 5.1 %copy-start.1 = (bf16[3584,16]{0,1:T(8,128)(2,1)S(1)}, bf16[3584,16]{0,1:T(8,128)(2,1)}, u32[]{:S(2)}) copy-start(bf16[3584,16]{0,1:T(8,128)(2,1)} %param.15) | copy-start | bytes 344068
  7.6 4.9 %copy-start.2 = (bf16[2,8,3584]{2,1,0:T(8,128)(2,1)S(1)}, bf16[2,8,3584]{2,1,0:T(8,128)(2,1)}, u32[]{:S(2)}) copy-start(bf16[2,8,3584]{2,1,0:T(8,128)(2,1)} %param.11) | copy-start | bytes 344068
  12.4 1.4 %collective-permute-start = (f32[64,512]{1,0:T(8,128)S(1)}, f32[64,512]{1,0:T(8,128)S(1)}, u32[]{:S(2)}, u32[]{:S(2)}) collective-permute-start(f32[64,512]{1,0:T(8,128)S(1)} %copy.17.own_ref.feats_ref), channel_id=1, source_target_pairs={{0,1},{1,0},{2,3},{3,2},{4,5},{5,4},{6,7},{7,6},{8,9},{9,8},{10,11... | collective-permute-start | bytes 393224 | tf_op jit(solution)/shard_map/ppermute | solution.py:42
  14.6 6.3 %collective-permute-start.1 = (f32[160,128]{1,0:T(8,128)S(1)}, f32[160,128]{1,0:T(8,128)S(1)}, u32[]{:S(2)}, u32[]{:S(2)}) collective-permute-start(f32[160,128]{1,0:T(8,128)S(1)} %get-tuple-element.10), channel_id=1, source_target_pairs={{0,64},{8,72},{16,80},{24,88},{32,96},{40,104},{48,112},{56,120},{... | collective-permute-start | bytes 245768 | tf_op jit(solution)/shard_map/ppermute | solution.py:42
  16.2 7.1 %collective-permute-start.2 = (f32[160,128]{1,0:T(8,128)S(1)}, f32[160,128]{1,0:T(8,128)S(1)}, u32[]{:S(2)}, u32[]{:S(2)}) collective-permute-start(f32[160,128]{1,0:T(8,128)S(1)} %get-tuple-element.11), channel_id=1, source_target_pairs={{0,128},{8,136},{16,144},{24,152},{32,160},{40,168},{48,176},{56,1... | collective-permute-start | bytes 245768 | tf_op jit(solution)/shard_map/ppermute | solution.py:42
  19.1 4.4 %collective-permute-start.3 = (f32[160,128]{1,0:T(8,128)S(1)}, f32[160,128]{1,0:T(8,128)S(1)}, u32[]{:S(2)}, u32[]{:S(2)}) collective-permute-start(f32[160,128]{1,0:T(8,128)S(1)} %get-tuple-element.12), channel_id=1, source_target_pairs={{0,192},{8,200},{16,208},{24,216},{32,224},{40,232},{48,240},{56,2... | collective-permute-start | bytes 245768 | tf_op jit(solution)/shard_map/ppermute | solution.py:42
  23.6 4.6 %collective-permute-start.4 = (f32[168,128]{1,0:T(8,128)S(1)}, f32[168,128]{1,0:T(8,128)S(1)}, u32[]{:S(2)}, u32[]{:S(2)}) collective-permute-start(f32[168,128]{1,0:T(8,128)S(1)} %pad_maximum_fusion.1), channel_id=1, source_target_pairs={{0,8},{8,0},{16,24},{24,16},{32,40},{40,32},{48,56},{56,48},{64,72... | collective-permute-start | bytes 258056 | tf_op jit(solution)/shard_map/ppermute | solution.py:42
  28.2 10.5 %collective-permute-start.5 = (f32[176,128]{1,0:T(8,128)S(1)}, f32[176,128]{1,0:T(8,128)S(1)}, u32[]{:S(2)}, u32[]{:S(2)}) collective-permute-start(f32[176,128]{1,0:T(8,128)S(1)} %pad_maximum_fusion), channel_id=1, source_target_pairs={{0,16},{8,24},{16,32},{24,40},{32,48},{40,56},{48,0},{56,8},{64,80... | collective-permute-start | bytes 270344 | tf_op jit(solution)/shard_map/ppermute | solution.py:42
  31.6 8.3 %collective-permute-start.6 = (f32[176,128]{1,0:T(8,128)S(1)}, f32[176,128]{1,0:T(8,128)S(1)}, u32[]{:S(2)}, u32[]{:S(2)}) collective-permute-start(f32[176,128]{1,0:T(8,128)S(1)} %pad_maximum_fusion), channel_id=1, source_target_pairs={{0,48},{8,56},{16,0},{24,8},{32,16},{40,24},{48,32},{56,40},{64,11... | collective-permute-start | bytes 270344 | tf_op jit(solution)/shard_map/ppermute | solution.py:42
  33.9 10.3 %collective-permute-start.7 = (f32[176,128]{1,0:T(8,128)S(1)}, f32[176,128]{1,0:T(8,128)S(1)}, u32[]{:S(2)}, u32[]{:S(2)}) collective-permute-start(f32[176,128]{1,0:T(8,128)S(1)} %pad_maximum_fusion), channel_id=1, source_target_pairs={{0,32},{8,40},{16,48},{24,56},{32,0},{40,8},{48,16},{56,24},{64,96... | collective-permute-start | bytes 270344 | tf_op jit(solution)/shard_map/ppermute | solution.py:42
  44.3 6.1 %collective-permute-start.8 = (f32[224,128]{1,0:T(8,128)S(1)}, f32[224,128]{1,0:T(8,128)S(1)}, u32[]{:S(2)}, u32[]{:S(2)}) collective-permute-start(f32[224,128]{1,0:T(8,128)S(1)} %get-tuple-element.15), channel_id=1, source_target_pairs={{0,64},{8,72},{16,80},{24,88},{32,96},{40,104},{48,112},{56,120},{... | collective-permute-start | bytes 344072 | tf_op jit(solution)/shard_map/ppermute | solution.py:42
  45.1 7.0 %collective-permute-start.9 = (f32[224,128]{1,0:T(8,128)S(1)}, f32[224,128]{1,0:T(8,128)S(1)}, u32[]{:S(2)}, u32[]{:S(2)}) collective-permute-start(f32[224,128]{1,0:T(8,128)S(1)} %get-tuple-element.15), channel_id=1, source_target_pairs={{0,128},{8,136},{16,144},{24,152},{32,160},{40,168},{48,176},{56,1... | collective-permute-start | bytes 344072 | tf_op jit(solution)/shard_map/ppermute | solution.py:42
  48.1 4.8 %collective-permute-start.10 = (f32[224,128]{1,0:T(8,128)S(1)}, f32[224,128]{1,0:T(8,128)S(1)}, u32[]{:S(2)}, u32[]{:S(2)}) collective-permute-start(f32[224,128]{1,0:T(8,128)S(1)} %get-tuple-element.15), channel_id=1, source_target_pairs={{0,192},{8,200},{16,208},{24,216},{32,224},{40,232},{48,240},{56,2... | collective-permute-start | bytes 344072 | tf_op jit(solution)/shard_map/ppermute | solution.py:42
  52.9 1.9 %collective-permute-start.11 = (f32[896,128]{1,0:T(8,128)S(1)}, f32[896,128]{1,0:T(8,128)S(1)}, u32[]{:S(2)}, u32[]{:S(2)}) collective-permute-start(f32[896,128]{1,0:T(8,128)S(1)} %constant_dynamic-update-slice_fusion.6.own_ref), channel_id=1, source_target_pairs={{0,1},{1,0},{2,3},{3,2},{4,5},{5,4},{6,7},{7,6},{8,9},{9,8},{10,11... | collective-permute-start | bytes 1376264 | tf_op jit(solution)/shard_map/ppermute | solution.py:42
  74.2 4.8 %collective-permute-start.12 = (f32[64,128]{1,0:T(8,128)S(1)}, f32[64,128]{1,0:T(8,128)S(1)}, u32[]{:S(2)}, u32[]{:S(2)}) collective-permute-start(f32[64,128]{1,0:T(8,128)S(1)} %shard_map.83), channel_id=1, source_target_pairs={{0,2},{2,0},{4,6},{6,4},{1,3},{3,1},{5,7},{7,5},{8,10},{10,8},{12,... | collective-permute-start | bytes 98312 | tf_op jit(solution)/shard_map/ppermute | solution.py:42
  75.7 5.4 %collective-permute-start.13 = (f32[64,128]{1,0:T(8,128)S(1)}, f32[64,128]{1,0:T(8,128)S(1)}, u32[]{:S(2)}, u32[]{:S(2)}) collective-permute-start(f32[64,128]{1,0:T(8,128)S(1)} %shard_map.83), channel_id=1, source_target_pairs={{0,4},{2,6},{4,0},{6,2},{1,5},{3,7},{5,1},{7,3},{8,12},{10,14},{12... | collective-permute-start | bytes 98312 | tf_op jit(solution)/shard_map/ppermute | solution.py:42
  78.5 5.1 %collective-permute-start.14 = (f32[64,128]{1,0:T(8,128)S(1)}, f32[64,128]{1,0:T(8,128)S(1)}, u32[]{:S(2)}, u32[]{:S(2)}) collective-permute-start(f32[64,128]{1,0:T(8,128)S(1)} %shard_map.83), channel_id=1, source_target_pairs={{0,6},{2,4},{4,2},{6,0},{1,7},{3,5},{5,3},{7,1},{8,14},{10,12},{12... | collective-permute-start | bytes 98312 | tf_op jit(solution)/shard_map/ppermute | solution.py:42

commit v2 on v1

--- a/solution.py
+++ b/solution.py
@@ -8,12 +8,16 @@
 from jax.sharding import PartitionSpec as P
 
 D = 4096
-OUTB = 2
 K1 = 32
 K2 = 16
 KB = 512
 RANK = 8
 EXAMPLES = 4096
+NBLOCKS = 128
+BLOCK_ROWS = 32
+CHUNKS = 1
+PARTS = 2
+LATER = 8
 RIDGE = 1.0
 TILE = 128
 PANEL = 16
@@ -25,6 +29,7 @@
 CHUNK = HALF * TILE // NY
 HIGH = lax.Precision.HIGHEST
 VMEM_LIMIT = 48 << 20
+VMEM_WHOLE = 40 << 20
 
 
 def dot(a, b, contract=(1, 0)):
@@ -50,39 +55,163 @@
     return move(block, "examples", lambda e: e // NZ * NZ + (e % NZ + step) % NZ)
 
 
-def build_map(block_maps, block_index, block_sign):
-    chooser = (block_index[:, None] == jnp.arange(OUTB, dtype=jnp.int32)[None, :]).astype(
-        jnp.float32
-    )
-    chooser = chooser * (2 * block_sign - 1).astype(jnp.float32)[:, None]
-    dense = block_maps.astype(jnp.float32)[:, :, None, :] * chooser[:, None, :, None]
-    return dense.reshape(D, K1).astype(jnp.bfloat16)
-
-
-def features(inputs, grad_rows, input_map, ff_part):
-    row_count = inputs.shape[0]
-    left_part = jnp.dot(
-        inputs.reshape(row_count * RANK, D), input_map, preferred_element_type=jnp.float32
-    )
-    right_part = jnp.dot(
-        grad_rows.reshape(row_count * RANK, grad_rows.shape[2]),
-        ff_part,
-        preferred_element_type=jnp.float32,
-    )
-    outer = jnp.einsum(
-        "erk,erl->ekl",
-        left_part.reshape(row_count, RANK, K1),
-        right_part.reshape(row_count, RANK, K2),
-        precision=HIGH,
-    )
-    return outer.reshape(row_count, K1 * K2) / math.sqrt(RANK)
-
-
-def lookup(table, index):
-    value = jnp.int32(table[0])
-    for place, entry in enumerate(table[1:], 1):
-        value = jnp.where(index == place, jnp.int32(entry), value)
-    return value
+def split(value):
+    high = value.astype(jnp.bfloat16)
+    rest = value - high.astype(jnp.float32)
+    middle = rest.astype(jnp.bfloat16)
+    return high, middle, (rest - middle.astype(jnp.float32)).astype(jnp.bfloat16)
+
+
+def spread_parts(value):
+    high, middle, low = (part.astype(jnp.float32) for part in split(value))
+    first = high + pltpu.roll(middle, 64, 1)
+    return jnp.concatenate([first, low], 1).astype(jnp.bfloat16)
+
+
+def feature_kernel(*refs):
+    sources, feats_ref, query_ref = refs[:8], refs[8], refs[9]
+    index_ref, sign_ref, maps_ref, ff_ref, grads_ref, inputs_ref = refs[10:16]
+    dense, weights, ff_weights, total, right_total, arrived = refs[16:]
+    index_hbm, sign_hbm, maps_hbm, ff_hbm, query_grads_hbm, grads_hbm, query_hbm, inputs_hbm = sources
+    main = inputs_hbm.shape[0]
+    rows = inputs_ref.shape[0]
+    plan = [
+        (index_hbm, index_ref),
+        (sign_hbm, sign_ref),
+        (ff_hbm, ff_ref),
+        (maps_hbm, maps_ref),
+        (query_grads_hbm, grads_ref.at[main:rows, :]),
+        (grads_hbm, grads_ref.at[0:main, :]),
+        (query_hbm, inputs_ref.at[main:rows, :]),
+    ]
+    width = inputs_ref.shape[1] // CHUNKS
+    for k in range(CHUNKS):
+        part = slice(k * width, (k + 1) * width)
+        plan.append((inputs_hbm.at[:, part], inputs_ref.at[0:main, part]))
+    copies = [
+        pltpu.make_async_copy(source, target, arrived.at[k])
+        for k, (source, target) in enumerate(plan)
+    ]
+    for copy in copies[:6]:
+        copy.start()
+
+    def iota(shape, axis):
+        return lax.broadcasted_iota(jnp.int32, shape, axis)
+
+    for copy in copies[:3]:
+        copy.wait()
+    place = (iota((K2, TILE), 1) - K1 == iota((K2, TILE), 0)).astype(jnp.bfloat16)
+    ff_weights[...] = lax.dot_general(
+        ff_ref[...], place, (((0,), (0,)), ((), ())), preferred_element_type=jnp.float32
+    ).astype(jnp.bfloat16)
+
+    copies[3].wait()
+    signs = 2 * sign_ref[...] - 1
+    chooser = [
+        jnp.where(index_ref[...] == c, signs, 0).astype(jnp.float32) for c in range(K1 // K2)
+    ]
+    groups = TILE // K1
+    group = iota((NBLOCKS, TILE), 1) // K1
+    for first in range(0, BLOCK_ROWS, groups):
+        if first == LATER:
+            for copy in copies[6:]:
+                copy.start()
+        stack = []
+        for i in range(first, first + groups):
+            values = maps_ref[i].astype(jnp.float32)
+            stack += [values * factor for factor in chooser]
+        turned = jnp.concatenate(stack, 0).T
+        for g in range(groups):
+            dense[pl.ds(first + g, NBLOCKS, stride=BLOCK_ROWS), :] = jnp.where(
+                group == g, turned, 0.0
+            )
+    weights[...] = dense[...].astype(jnp.bfloat16)
+
+    def project(values_ref, weights_ref, out_ref):
+        depth = values_ref.shape[1] // PARTS
+
+        def body(k, carry):
+            part = pl.ds(pl.multiple_of(k * depth, TILE), depth)
+            out_ref[...] += jnp.dot(
+                values_ref[:, part], weights_ref[part, :], preferred_element_type=jnp.float32
+            )
+            return carry
+
+        out_ref[...] = jnp.zeros_like(out_ref)
+        lax.fori_loop(0, PARTS, body, 0)
+
+    copies[4].wait()
+    copies[5].wait()
+    project(grads_ref, ff_weights, right_total)
+    for copy in copies[6:]:
+        copy.wait()
+    project(inputs_ref, weights, total)
+    left = total[...]
+    left = left + pltpu.roll(left, 2 * K1, 1)
+    left = left + pltpu.roll(left, K1, 1)
+    total[...] = jnp.where(iota((rows, TILE), 1) < K1, left, right_total[...])
+
+    source = iota((2 * TILE, 2 * KB), 0) & 63
+    lanes = iota((2 * TILE, 2 * KB), 1)
+    from_left = (lanes < KB) & (source == lanes // K2)
+    from_right = (lanes >= KB) & (source == K1 + (lanes & (K2 - 1)))
+    used = iota((2 * TILE, 2 * KB), 0) < 3 * 64
+    expand = ((from_left | from_right) & used).astype(jnp.bfloat16)
+    count = feats_ref.shape[0]
+    by_rank = [total[pl.ds(r, count, stride=RANK), :] for r in range(RANK)]
+    by_rank.append(total[main:rows, :])
+    wide = jnp.dot(
+        spread_parts(jnp.concatenate(by_rank, 0)), expand, preferred_element_type=jnp.float32
+    )
+    product = wide[:, :KB] * wide[:, KB:]
+    value = product[:count]
+    for r in range(1, RANK):
+        value = value + product[r * count : (r + 1) * count]
+    feats_ref[...] = value * (1.0 / math.sqrt(RANK))
+    for i in range((rows - main) // RANK):
+        first = main + i * RANK
+        row = jnp.sum(product[first : first + RANK], 0, keepdims=True) * (1.0 / math.sqrt(RANK))
+        for c in range(NB):
+            at = 2 * c + i
+            query_ref[at : at + 1, :] = row[:, c * TILE : (c + 1) * TILE]
+
+
+def features(train, grads, query, query_grads, block_maps, block_index, block_sign, ff_map):
+    count = train.shape[0]
+    train, grads, query, query_grads = (
+        x.reshape(-1, x.shape[-1]) for x in (train, grads, query, query_grads)
+    )
+    operands = [
+        block_index.reshape(1, -1),
+        block_sign.reshape(1, -1),
+        block_maps.transpose(1, 2, 0),
+        ff_map.T,
+        query_grads,
+        grads,
+        query,
+        train,
+    ]
+    rows = train.shape[0] + query.shape[0]
+    return pl.pallas_call(
+        feature_kernel,
+        in_specs=[pl.BlockSpec(memory_space=pltpu.HBM)] * len(operands),
+        out_shape=[
+            jax.ShapeDtypeStruct((count, KB), jnp.float32),
+            jax.ShapeDtypeStruct((2 * NB, TILE), jnp.float32),
+        ],
+        scratch_shapes=[pltpu.VMEM(x.shape, x.dtype) for x in operands[:4]]
+        + [
+            pltpu.VMEM((rows, grads.shape[1]), jnp.bfloat16),
+            pltpu.VMEM((rows, D), jnp.bfloat16),
+            pltpu.VMEM((D, TILE), jnp.float32),
+            pltpu.VMEM((D, TILE), jnp.bfloat16),
+            pltpu.VMEM((grads.shape[1], TILE), jnp.bfloat16),
+            pltpu.VMEM((rows, TILE), jnp.float32),
+            pltpu.VMEM((rows, TILE), jnp.float32),
+            pltpu.SemaphoreType.DMA((7 + CHUNKS,)),
+        ],
+        compiler_params=pltpu.CompilerParams(vmem_limit_bytes=VMEM_WHOLE),
+    )(*[pltpu.with_memory_space_constraint(x, pltpu.HBM) for x in operands])
 
 
 def gram_kernel(own_ref, other_ref, keep_ref, first_ref, second_ref, third_ref, half):
@@ -118,19 +247,40 @@
     return rows
 
 
-def block_inverse(block):
-    lane = lax.broadcasted_iota(jnp.int32, (TILE, TILE), 1)
-    for first in range(0, TILE, PANEL):
-        last = first + PANEL
-        fresh = panel_inverse(block[first:last], first)
-        update = dot(block[:, first:last], fresh)
-        block = jnp.where((lane >= first) & (lane < last), 0.0, block) - update
-        parts = [block[:first]] if first else []
-        parts.append(fresh)
-        if last < TILE:
-            parts.append(block[last:])
-        block = jnp.concatenate(parts, 0)
-    return block
+def panel_update(rows, factors, first, fresh):
+    lane = lax.broadcasted_iota(jnp.int32, (PANEL, TILE), 1)
+    inside = (lane >= first) & (lane < first + PANEL)
+    even, odd = jnp.where(inside, 0.0, rows), None
+    for j in range(PANEL):
+        column = jnp.broadcast_to(factors[:, first + j : first + j + 1], (PANEL, TILE))
+        term = column * fresh[j : j + 1]
+        if j % 2 == 0:
+            even = even - term
+        else:
+            odd = term if odd is None else odd + term
+    return even - odd
+
+
+def block_inverse(block, between=lambda: None):
+    lane = lax.broadcasted_iota(jnp.int32, (PANEL, TILE), 1)
+    count = TILE // PANEL
+    rows = [block[i * PANEL : (i + 1) * PANEL] for i in range(count)]
+    fresh = None
+    for t in range(count):
+        first = t * PANEL
+        current = rows[t]
+        if t:
+            current = panel_update(current, current, first - PANEL, fresh)
+        fresh = panel_inverse(current, first)
+        others = [i for i in range(count) if i not in (t, t + 1)]
+        factors = jnp.concatenate([rows[i] for i in others], 0)[:, first : first + PANEL]
+        update = dot(factors, fresh)
+        inside = (lane >= first) & (lane < first + PANEL)
+        for k, i in enumerate(others):
+            rows[i] = jnp.where(inside, 0.0, rows[i]) - update[k * PANEL : (k + 1) * PANEL]
+        rows[t] = fresh
+        between()
+    return jnp.concatenate(rows, 0)
 
 
 def solve_kernel(own_ref, other_ref, feats_ref, out_ref, gram, query):
@@ -152,15 +302,21 @@
     r = lax.broadcasted_iota(jnp.int32, (total_rows, TILE), 0)
     n = lax.broadcasted_iota(jnp.int32, (total_rows, TILE), 1)
     side, step = r >> 8, (r >> 6) & 3
-    group, pair, item, part = (r >> 4) & 3, (r >> 3) & 1, (r >> 2) & 1, r & 3
+    group, pair, part, item = (r >> 4) & 3, (r >> 3) & 1, (r >> 1) & 3, r & 1
     shift = jnp.where(group == 0, 0, jnp.where(group == 1, 6, jnp.where(group == 2, 2, 4)))
     source_z = ((z + shift) & 7) ^ pair
     source_y = (y + 4 - step) & 3
     source = (((source_y * NZ + source_z) * 2 + (side ^ rep)) * 2) + item
-    values = query[...]
-    right = [
-        dot(values, ((source == n) & (part == c)).astype(jnp.float32), (0, 0)) for c in range(NB)
-    ]
+    right = [None] * NB
+
+    def pick(c):
+        chosen = ((source == n) & (part == c)).astype(jnp.bfloat16)
+        right[c] = sum(
+            lax.dot_general(
+                piece, chosen, (((0,), (0,)), ((), ())), preferred_element_type=jnp.float32
+            )
+            for piece in split(query[...])
+        )
 
     eye = (
         lax.broadcasted_iota(jnp.int32, (TILE, TILE), 0)
@@ -172,22 +328,47 @@
         block[i, j] = value + eye if i == j else value
 
     solved = []
+    pending = [lambda c=c: pick(c) for c in range(NB)]
+
+    def between():
+        if pending:
+            pending.pop(0)()
+
     for b in range(NB):
-        inverse = block_inverse(block[b, b])
-        wide = jnp.concatenate([block[b, j] for j in range(b + 1, NB)] + [right[b]], 1)
-        done = dot(inverse, wide)
+        inverse = block_inverse(block[b, b], between)
+        while pending:
+            between()
+        if b == NB - 1:
+            solved.append([dot(inverse, right[b])])
+            break
+        near = dot(inverse, block[b, b + 1])
+        block[b + 1, b + 1] = block[b + 1, b + 1] - dot(block[b, b + 1], near, (0, 0))
+        done = [near]
         solved.append(done)
+
+        def finish(b=b, done=done, inverse=inverse):
+            width = NB - 2 - b
+            wide = jnp.concatenate([block[b, j] for j in range(b + 2, NB)] + [right[b]], 1)
+            wide = dot(inverse, wide)
+            done += [wide[:, k * TILE : (k + 1) * TILE] for k in range(width + 1)]
+
+        def trail(i, b=b, done=done):
+            first = max(i, b + 2)
+            change = dot(block[b, i], jnp.concatenate(done[first - b - 1 :], 1), (0, 0))
+            for j in range(first, NB):
+                at = (j - first) * TILE
+                block[i, j] = block[i, j] - change[:, at : at + TILE]
+            right[i] = right[i] - change[:, (NB - first) * TILE :]
+
+        pending.append(finish)
         for i in range(b + 1, NB):
-            change = dot(block[b, i], done[:, (i - b - 1) * TILE :], (0, 0))
-            for j in range(i, NB):
-                block[i, j] = block[i, j] - change[:, (j - i) * TILE : (j - i + 1) * TILE]
-            right[i] = right[i] - change[:, (NB - i) * TILE :]
+            pending.append(lambda i=i, trail=trail: trail(i))
     answer = [None] * NB
     for b in reversed(range(NB)):
-        value = solved[b][:, (NB - 1 - b) * TILE :]
+        value = solved[b][NB - 1 - b]
         if b < NB - 1:
             later = jnp.concatenate(answer[b + 1 :], 0)
-            value = value - dot(solved[b][:, : (NB - 1 - b) * TILE], later)
+            value = value - dot(jnp.concatenate(solved[b][: NB - 1 - b], 1), later)
         answer[b] = value
     out_ref[...] = dot(feats_ref[...], jnp.concatenate(answer, 0)) * (1.0 / math.sqrt(4 * KB))
 
@@ -202,9 +383,16 @@
     block_sign,
     ff_map,
 ):
-    input_map = build_map(block_maps, block_index, block_sign)
-    train_feats = features(train_inputs, train_grads, input_map, ff_map)
-    query_feats = features(query_inputs, query_grads, input_map, ff_map)
+    train_feats, query_feats = features(
+        train_inputs,
+        train_grads,
+        query_inputs,
+        query_grads,
+        block_maps,
+        block_index,
+        block_sign,
+        ff_map,
+    )
     other_feats = move(train_feats, "reps", lambda r: 1 - r)
     params = pltpu.CompilerParams(vmem_limit_bytes=VMEM_LIMIT)
     piece = jax.ShapeDtypeStruct((CHUNK, TILE), jnp.float32)
@@ -218,7 +406,7 @@
     first = along_y(first, 1)
     third = along_y(third, 3)
     gram = keep + first + second + third
-    held = jnp.concatenate([gram, query_feats.reshape(-1, TILE)], 0)
+    held = jnp.concatenate([gram, query_feats], 0)
     near = move(held, "examples", lambda e: e ^ 1)
     held = jnp.concatenate([gram + near[:CHUNK], held[CHUNK:], near[CHUNK:]], 0)
     far = along_z(held, 4)

time: 84.4 us -> 71.4 us (0.85)
  matrix products: 8.28 us -> 0 us
  local copies, waits for them, and re-layouts: 3.16 us -> 0.06 us
  starting transfers between devices: 27.3 us -> 25.3 us
  other arithmetic: 2.33 us -> 0.7 us
  waiting for transfers between devices: 22.8 us -> 24.1 us
  Pallas kernels: 20.1 us -> 21 us
    dot_general x6 -> x0, matrix products: 8.28 us -> none  [the longest x2 3.74 us: features(): jnp.dot(inputs.reshape(row_count * RANK, D), input_map, preferred_element...]
    pallas_call x0 -> x1, Pallas kernels: none -> 6.41 us  [features(): pl.pallas_call(feature_kernel, in_specs=[pl.BlockSpec(memory_space=pltpu....]
    pallas_call x1, Pallas kernels: 19.3 us -> 13.8 us  [on_device(): pl.pallas_call(solve_kernel, out_shape=jax.ShapeDtypeStruct((train_feats....]
    convert_element_type x2 -> x0, local copies, waits for them, and re-layouts: 2.39 us -> none  [the longest x1 1.29 us: build_map(): block_maps.astype(jnp.float32)[:, :, None, :] * chooser[:, None, :, None]]
    ppermute x15, starting transfers between devices: 27.3 us -> 25.3 us  [move(): return lax.ppermute(block, axis, [(i, target(i)) for i in range(count)])]
    ppermute x15, waiting for transfers between devices: 22.8 us -> 24.1 us  [move(): return lax.ppermute(block, axis, [(i, target(i)) for i in range(count)])]
    convert_element_type x2 -> x0, other arithmetic: 0.98 us -> none  [the longest x1 0.66 us: build_map(): chooser = chooser * (2 * block_sign - 1).astype(jnp.float32)[:, None]]
  transfers between devices with their start and end apart: 15 -> 15, of which waited for: 12 -> 11; matrix products, arithmetic and copies ran while one was open for 1% -> 0% of each run, Pallas kernels for 0% -> 0%
where the time goes in v2:
time: 71.4 us; the launch traced here: 71.3 us
  starting transfers between devices  25.3 us (35%)
  waiting for transfers between devices  24.1 us (34%)
  Pallas kernels  21 us (29%)
    ppermute x15, starting transfers between devices, move(): return lax.ppermute(block, axis, [(i, target(i)) for i in range(count)])  25.3 us
    ppermute x15, waiting for transfers between devices, move(): return lax.ppermute(block, axis, [(i, target(i)) for i in range(count)])  24.1 us
    pallas_call x1, Pallas kernels, on_device(): pl.pallas_call(solve_kernel, out_shape=jax.ShapeDtypeStruct((train_feats....  13.8 us
    pallas_call x1, Pallas kernels, features(): pl.pallas_call(feature_kernel, in_specs=[pl.BlockSpec(memory_space=pltpu....  6.41 us
  transfers between devices with their start and end apart: 15, of which 11 were waited for; matrix products, arithmetic and copies ran while one was open for 0% of the time, Pallas kernels for 0%

profile of v2, /device:TPU:32, one launch (start us, length us, event | category | flops | bytes accessed | tf_op | source)
XLA Modules:
  0.0 71.3 jit_solution(17910975194768788040)
XLA Ops:
  0.0 6.4 %shard_map.82 = (f32[64,512]{1,0:T(8,128)S(1)}, f32[8,128]{1,0:T(8,128)S(1)}) custom-call(s32[1,128]{1,0:T(1,128)} %bitcast.14, s32[1,128]{1,0:T(1,128)} %bitcast.15, bf16[32,16,128]{2,1,0:T(8,128)(2,1)} %bitcast.10, bf16[16,3584]{1,0:T(8,128)(2,1)} %bitcast.12, bf16[16,3584]{1,0:T(8,128)(2,1)} %bitcast.13, bf16[512,3584]{1,0:T(8,128)(2,1)} %bitcast.9, ...), custom_call_target="tpu_custom_call" | custom-call | tf_op jit(solution)/shard_map/pallas_call | solution.py:195
  6.5 1.3 %collective-permute-done.other_ref = f32[64,512]{1,0:T(8,128)S(1)} collective-permute-done((f32[64,512]{1,0:T(8,128)S(1)}, f32[64,512]{1,0:T(8,128)S(1)}, u32[]{:S(2)}, u32[]{:S(2)}) %collective-permute-start) | collective-permute-done | bytes 131104 | tf_op jit(solution)/shard_map/ppermute | solution.py:47
  7.9 0.8 %shard_map.83 = (f32[160,128]{1,0:T(8,128)S(1)}, f32[160,128]{1,0:T(8,128)S(1)}, f32[160,128]{1,0:T(8,128)S(1)}, f32[160,128]{1,0:T(8,128)S(1)}) custom-call(f32[64,512]{1,0:T(8,128)S(1)} %get-tuple-element.11.own_ref.feats_ref, f32[64,512]{1,0:T(8,128)S(1)} %collective-permute-done.other_ref), custom_call_target="tpu_custom_call" | custom-call | tf_op jit(solution)/shard_map/pallas_call | solution.py:399
  8.6 1.6 %collective-permute-start.1 = (f32[160,128]{1,0:T(8,128)S(1)}, f32[160,128]{1,0:T(8,128)S(1)}, u32[]{:S(2)}, u32[]{:S(2)}) collective-permute-start(f32[160,128]{1,0:T(8,128)S(1)} %get-tuple-element.13), channel_id=1, source_target_pairs={{0,64},{8,72},{16,80},{24,88},{32,96},{40,104},{48,112},{56,120},{... | collective-permute-start | bytes 245768 | tf_op jit(solution)/shard_map/ppermute | solution.py:47
  10.3 2.9 %collective-permute-start.2 = (f32[160,128]{1,0:T(8,128)S(1)}, f32[160,128]{1,0:T(8,128)S(1)}, u32[]{:S(2)}, u32[]{:S(2)}) collective-permute-start(f32[160,128]{1,0:T(8,128)S(1)} %get-tuple-element.14), channel_id=1, source_target_pairs={{0,128},{8,136},{16,144},{24,152},{32,160},{40,168},{48,176},{56,1... | collective-permute-start | bytes 245768 | tf_op jit(solution)/shard_map/ppermute | solution.py:47
  13.2 1.3 %collective-permute-start.3 = (f32[160,128]{1,0:T(8,128)S(1)}, f32[160,128]{1,0:T(8,128)S(1)}, u32[]{:S(2)}, u32[]{:S(2)}) collective-permute-start(f32[160,128]{1,0:T(8,128)S(1)} %get-tuple-element.15), channel_id=1, source_target_pairs={{0,192},{8,200},{16,208},{24,216},{32,224},{40,232},{48,240},{56,2... | collective-permute-start | bytes 245768 | tf_op jit(solution)/shard_map/ppermute | solution.py:47
  14.5 2.9 %collective-permute-done.2 = f32[160,128]{1,0:T(8,128)S(1)} collective-permute-done((f32[160,128]{1,0:T(8,128)S(1)}, f32[160,128]{1,0:T(8,128)S(1)}, u32[]{:S(2)}, u32[]{:S(2)}) %collective-permute-start.2) | collective-permute-done | bytes 81952 | tf_op jit(solution)/shard_map/ppermute | solution.py:47
  17.7 1.1 %collective-permute-start.4 = (f32[168,128]{1,0:T(8,128)S(1)}, f32[168,128]{1,0:T(8,128)S(1)}, u32[]{:S(2)}, u32[]{:S(2)}) collective-permute-start(f32[168,128]{1,0:T(8,128)S(1)} %pad_maximum_fusion.1), channel_id=1, source_target_pairs={{0,8},{8,0},{16,24},{24,16},{32,40},{40,32},{48,56},{56,48},{64,72... | collective-permute-start | bytes 258056 | tf_op jit(solution)/shard_map/ppermute | solution.py:47
  18.7 3.5 %collective-permute-done.4 = f32[168,128]{1,0:T(8,128)S(1)} collective-permute-done((f32[168,128]{1,0:T(8,128)S(1)}, f32[168,128]{1,0:T(8,128)S(1)}, u32[]{:S(2)}, u32[]{:S(2)}) %collective-permute-start.4) | collective-permute-done | bytes 86048 | tf_op jit(solution)/shard_map/ppermute | solution.py:47
  22.3 6.5 %collective-permute-start.7 = (f32[176,128]{1,0:T(8,128)S(1)}, f32[176,128]{1,0:T(8,128)S(1)}, u32[]{:S(2)}, u32[]{:S(2)}) collective-permute-start(f32[176,128]{1,0:T(8,128)S(1)} %pad_maximum_fusion), channel_id=1, source_target_pairs={{0,32},{8,40},{16,48},{24,56},{32,0},{40,8},{48,16},{56,24},{64,96... | collective-permute-start | bytes 270344 | tf_op jit(solution)/shard_map/ppermute | solution.py:47
  29.2 2.4 %collective-permute-start.5 = (f32[176,128]{1,0:T(8,128)S(1)}, f32[176,128]{1,0:T(8,128)S(1)}, u32[]{:S(2)}, u32[]{:S(2)}) collective-permute-start(f32[176,128]{1,0:T(8,128)S(1)} %pad_maximum_fusion), channel_id=1, source_target_pairs={{0,16},{8,24},{16,32},{24,40},{32,48},{40,56},{48,0},{56,8},{64,80... | collective-permute-start | bytes 270344 | tf_op jit(solution)/shard_map/ppermute | solution.py:47
  31.7 3.0 %collective-permute-done.6 = f32[176,128]{1,0:T(8,128)S(1)} collective-permute-done((f32[176,128]{1,0:T(8,128)S(1)}, f32[176,128]{1,0:T(8,128)S(1)}, u32[]{:S(2)}, u32[]{:S(2)}) %collective-permute-start.6) | collective-permute-done | bytes 90144 | tf_op jit(solution)/shard_map/ppermute | solution.py:47
  34.6 2.1 %collective-permute-done.5 = f32[176,128]{1,0:T(8,128)S(1)} collective-permute-done((f32[176,128]{1,0:T(8,128)S(1)}, f32[176,128]{1,0:T(8,128)S(1)}, u32[]{:S(2)}, u32[]{:S(2)}) %collective-permute-start.5) | collective-permute-done | bytes 90144 | tf_op jit(solution)/shard_map/ppermute | solution.py:47
  36.9 1.3 %collective-permute-start.8 = (f32[224,128]{1,0:T(8,128)S(1)}, f32[224,128]{1,0:T(8,128)S(1)}, u32[]{:S(2)}, u32[]{:S(2)}) collective-permute-start(f32[224,128]{1,0:T(8,128)S(1)} %get-tuple-element.19), channel_id=1, source_target_pairs={{0,64},{8,72},{16,80},{24,88},{32,96},{40,104},{48,112},{56,120},{... | collective-permute-start | bytes 344072 | tf_op jit(solution)/shard_map/ppermute | solution.py:47
  38.2 2.0 %collective-permute-start.10 = (f32[224,128]{1,0:T(8,128)S(1)}, f32[224,128]{1,0:T(8,128)S(1)}, u32[]{:S(2)}, u32[]{:S(2)}) collective-permute-start(f32[224,128]{1,0:T(8,128)S(1)} %get-tuple-element.19), channel_id=1, source_target_pairs={{0,192},{8,200},{16,208},{24,216},{32,224},{40,232},{48,240},{56,2... | collective-permute-start | bytes 344072 | tf_op jit(solution)/shard_map/ppermute | solution.py:47
  40.2 1.1 %collective-permute-start.9 = (f32[224,128]{1,0:T(8,128)S(1)}, f32[224,128]{1,0:T(8,128)S(1)}, u32[]{:S(2)}, u32[]{:S(2)}) collective-permute-start(f32[224,128]{1,0:T(8,128)S(1)} %get-tuple-element.19), channel_id=1, source_target_pairs={{0,128},{8,136},{16,144},{24,152},{32,160},{40,168},{48,176},{56,1... | collective-permute-start | bytes 344072 | tf_op jit(solution)/shard_map/ppermute | solution.py:47
  41.3 2.1 %collective-permute-done.8 = f32[224,128]{1,0:T(8,128)S(1)} collective-permute-done((f32[224,128]{1,0:T(8,128)S(1)}, f32[224,128]{1,0:T(8,128)S(1)}, u32[]{:S(2)}, u32[]{:S(2)}) %collective-permute-start.8) | collective-permute-done | bytes 114720 | tf_op jit(solution)/shard_map/ppermute | solution.py:47
  43.4 3.0 %collective-permute-done.9 = f32[224,128]{1,0:T(8,128)S(1)} collective-permute-done((f32[224,128]{1,0:T(8,128)S(1)}, f32[224,128]{1,0:T(8,128)S(1)}, u32[]{:S(2)}, u32[]{:S(2)}) %collective-permute-start.9) | collective-permute-done | bytes 114720 | tf_op jit(solution)/shard_map/ppermute | solution.py:47
  46.8 1.8 %collective-permute-done.11.other_ref = f32[896,128]{1,0:T(8,128)S(1)} collective-permute-done((f32[896,128]{1,0:T(8,128)S(1)}, f32[896,128]{1,0:T(8,128)S(1)}, u32[]{:S(2)}, u32[]{:S(2)}) %collective-permute-start.11) | collective-permute-done | bytes 458784 | tf_op jit(solution)/shard_map/ppermute | solution.py:47
  48.6 13.8 %shard_map.84 = f32[64,128]{1,0:T(8,128)S(1)} custom-call(f32[896,128]{1,0:T(8,128)S(1)} %constant_dynamic-update-slice_fusion.6.own_ref, f32[896,128]{1,0:T(8,128)S(1)} %collective-permute-done.11.other_ref, f32[64,512]{1,0:T(8,128)S(1)} %get-tuple-element.11.own_ref.feats_ref), custom_call_target="tpu_custom_call" | custom-call | tf_op jit(solution)/shard_map/pallas_call | solution.py:422
  62.4 2.8 %collective-permute-start.14 = (f32[64,128]{1,0:T(8,128)S(1)}, f32[64,128]{1,0:T(8,128)S(1)}, u32[]{:S(2)}, u32[]{:S(2)}) collective-permute-start(f32[64,128]{1,0:T(8,128)S(1)} %shard_map.84), channel_id=1, source_target_pairs={{0,6},{2,4},{4,2},{6,0},{1,7},{3,5},{5,3},{7,1},{8,14},{10,12},{12... | collective-permute-start | bytes 98312 | tf_op jit(solution)/shard_map/ppermute | solution.py:47
  65.2 0.8 %collective-permute-start.13 = (f32[64,128]{1,0:T(8,128)S(1)}, f32[64,128]{1,0:T(8,128)S(1)}, u32[]{:S(2)}, u32[]{:S(2)}) collective-permute-start(f32[64,128]{1,0:T(8,128)S(1)} %shard_map.84), channel_id=1, source_target_pairs={{0,4},{2,6},{4,0},{6,2},{1,5},{3,7},{5,1},{7,3},{8,12},{10,14},{12... | collective-permute-start | bytes 98312 | tf_op jit(solution)/shard_map/ppermute | solution.py:47
  66.6 1.0 %collective-permute-done.14 = f32[64,128]{1,0:T(8,128)S(1)} collective-permute-done((f32[64,128]{1,0:T(8,128)S(1)}, f32[64,128]{1,0:T(8,128)S(1)}, u32[]{:S(2)}, u32[]{:S(2)}) %collective-permute-start.14) | collective-permute-done | bytes 32800 | tf_op jit(solution)/shard_map/ppermute | solution.py:47
  67.6 3.1 %collective-permute-done.13 = f32[64,128]{1,0:T(8,128)S(1)} collective-permute-done((f32[64,128]{1,0:T(8,128)S(1)}, f32[64,128]{1,0:T(8,128)S(1)}, u32[]{:S(2)}, u32[]{:S(2)}) %collective-permute-start.13) | collective-permute-done | bytes 32800 | tf_op jit(solution)/shard_map/ppermute | solution.py:47
  (25 shorter events, 2.4 us)
Async XLA Ops:
  6.4 1.4 %collective-permute-start = (f32[64,512]{1,0:T(8,128)S(1)}, f32[64,512]{1,0:T(8,128)S(1)}, u32[]{:S(2)}, u32[]{:S(2)}) collective-permute-start(f32[64,512]{1,0:T(8,128)S(1)} %get-tuple-element.11.own_ref.feats_ref), channel_id=1, source_target_pairs={{0,1},{1,0},{2,3},{3,2},{4,5},{5,4},{6,7},{7,6},{8,9},{9,8},{10,11... | collective-permute-start | bytes 393224 | tf_op jit(solution)/shard_map/ppermute | solution.py:47
  8.6 5.9 %collective-permute-start.1 = (f32[160,128]{1,0:T(8,128)S(1)}, f32[160,128]{1,0:T(8,128)S(1)}, u32[]{:S(2)}, u32[]{:S(2)}) collective-permute-start(f32[160,128]{1,0:T(8,128)S(1)} %get-tuple-element.13), channel_id=1, source_target_pairs={{0,64},{8,72},{16,80},{24,88},{32,96},{40,104},{48,112},{56,120},{... | collective-permute-start | bytes 245768 | tf_op jit(solution)/shard_map/ppermute | solution.py:47
  10.3 7.1 %collective-permute-start.2 = (f32[160,128]{1,0:T(8,128)S(1)}, f32[160,128]{1,0:T(8,128)S(1)}, u32[]{:S(2)}, u32[]{:S(2)}) collective-permute-start(f32[160,128]{1,0:T(8,128)S(1)} %get-tuple-element.14), channel_id=1, source_target_pairs={{0,128},{8,136},{16,144},{24,152},{32,160},{40,168},{48,176},{56,1... | collective-permute-start | bytes 245768 | tf_op jit(solution)/shard_map/ppermute | solution.py:47
  13.2 4.4 %collective-permute-start.3 = (f32[160,128]{1,0:T(8,128)S(1)}, f32[160,128]{1,0:T(8,128)S(1)}, u32[]{:S(2)}, u32[]{:S(2)}) collective-permute-start(f32[160,128]{1,0:T(8,128)S(1)} %get-tuple-element.15), channel_id=1, source_target_pairs={{0,192},{8,200},{16,208},{24,216},{32,224},{40,232},{48,240},{56,2... | collective-permute-start | bytes 245768 | tf_op jit(solution)/shard_map/ppermute | solution.py:47
  17.7 4.6 %collective-permute-start.4 = (f32[168,128]{1,0:T(8,128)S(1)}, f32[168,128]{1,0:T(8,128)S(1)}, u32[]{:S(2)}, u32[]{:S(2)}) collective-permute-start(f32[168,128]{1,0:T(8,128)S(1)} %pad_maximum_fusion.1), channel_id=1, source_target_pairs={{0,8},{8,0},{16,24},{24,16},{32,40},{40,32},{48,56},{56,48},{64,72... | collective-permute-start | bytes 258056 | tf_op jit(solution)/shard_map/ppermute | solution.py:47
  22.3 9.4 %collective-permute-start.7 = (f32[176,128]{1,0:T(8,128)S(1)}, f32[176,128]{1,0:T(8,128)S(1)}, u32[]{:S(2)}, u32[]{:S(2)}) collective-permute-start(f32[176,128]{1,0:T(8,128)S(1)} %pad_maximum_fusion), channel_id=1, source_target_pairs={{0,32},{8,40},{16,48},{24,56},{32,0},{40,8},{48,16},{56,24},{64,96... | collective-permute-start | bytes 270344 | tf_op jit(solution)/shard_map/ppermute | solution.py:47
  28.7 5.9 %collective-permute-start.6 = (f32[176,128]{1,0:T(8,128)S(1)}, f32[176,128]{1,0:T(8,128)S(1)}, u32[]{:S(2)}, u32[]{:S(2)}) collective-permute-start(f32[176,128]{1,0:T(8,128)S(1)} %pad_maximum_fusion), channel_id=1, source_target_pairs={{0,48},{8,56},{16,0},{24,8},{32,16},{40,24},{48,32},{56,40},{64,11... | collective-permute-start | bytes 270344 | tf_op jit(solution)/shard_map/ppermute | solution.py:47
  29.2 7.6 %collective-permute-start.5 = (f32[176,128]{1,0:T(8,128)S(1)}, f32[176,128]{1,0:T(8,128)S(1)}, u32[]{:S(2)}, u32[]{:S(2)}) collective-permute-start(f32[176,128]{1,0:T(8,128)S(1)} %pad_maximum_fusion), channel_id=1, source_target_pairs={{0,16},{8,24},{16,32},{24,40},{32,48},{40,56},{48,0},{56,8},{64,80... | collective-permute-start | bytes 270344 | tf_op jit(solution)/shard_map/ppermute | solution.py:47
  36.9 6.6 %collective-permute-start.8 = (f32[224,128]{1,0:T(8,128)S(1)}, f32[224,128]{1,0:T(8,128)S(1)}, u32[]{:S(2)}, u32[]{:S(2)}) collective-permute-start(f32[224,128]{1,0:T(8,128)S(1)} %get-tuple-element.19), channel_id=1, source_target_pairs={{0,64},{8,72},{16,80},{24,88},{32,96},{40,104},{48,112},{56,120},{... | collective-permute-start | bytes 344072 | tf_op jit(solution)/shard_map/ppermute | solution.py:47
  38.2 8.3 %collective-permute-start.10 = (f32[224,128]{1,0:T(8,128)S(1)}, f32[224,128]{1,0:T(8,128)S(1)}, u32[]{:S(2)}, u32[]{:S(2)}) collective-permute-start(f32[224,128]{1,0:T(8,128)S(1)} %get-tuple-element.19), channel_id=1, source_target_pairs={{0,192},{8,200},{16,208},{24,216},{32,224},{40,232},{48,240},{56,2... | collective-permute-start | bytes 344072 | tf_op jit(solution)/shard_map/ppermute | solution.py:47
  40.2 6.3 %collective-permute-start.9 = (f32[224,128]{1,0:T(8,128)S(1)}, f32[224,128]{1,0:T(8,128)S(1)}, u32[]{:S(2)}, u32[]{:S(2)}) collective-permute-start(f32[224,128]{1,0:T(8,128)S(1)} %get-tuple-element.19), channel_id=1, source_target_pairs={{0,128},{8,136},{16,144},{24,152},{32,160},{40,168},{48,176},{56,1... | collective-permute-start | bytes 344072 | tf_op jit(solution)/shard_map/ppermute | solution.py:47
  46.5 2.1 %collective-permute-start.11 = (f32[896,128]{1,0:T(8,128)S(1)}, f32[896,128]{1,0:T(8,128)S(1)}, u32[]{:S(2)}, u32[]{:S(2)}) collective-permute-start(f32[896,128]{1,0:T(8,128)S(1)} %constant_dynamic-update-slice_fusion.6.own_ref), channel_id=1, source_target_pairs={{0,1},{1,0},{2,3},{3,2},{4,5},{5,4},{6,7},{7,6},{8,9},{9,8},{10,11... | collective-permute-start | bytes 1376264 | tf_op jit(solution)/shard_map/ppermute | solution.py:47
  62.4 5.2 %collective-permute-start.14 = (f32[64,128]{1,0:T(8,128)S(1)}, f32[64,128]{1,0:T(8,128)S(1)}, u32[]{:S(2)}, u32[]{:S(2)}) collective-permute-start(f32[64,128]{1,0:T(8,128)S(1)} %shard_map.84), channel_id=1, source_target_pairs={{0,6},{2,4},{4,2},{6,0},{1,7},{3,5},{5,3},{7,1},{8,14},{10,12},{12... | collective-permute-start | bytes 98312 | tf_op jit(solution)/shard_map/ppermute | solution.py:47
  65.2 5.4 %collective-permute-start.13 = (f32[64,128]{1,0:T(8,128)S(1)}, f32[64,128]{1,0:T(8,128)S(1)}, u32[]{:S(2)}, u32[]{:S(2)}) collective-permute-start(f32[64,128]{1,0:T(8,128)S(1)} %shard_map.84), channel_id=1, source_target_pairs={{0,4},{2,6},{4,0},{6,2},{1,5},{3,7},{5,1},{7,3},{8,12},{10,14},{12... | collective-permute-start | bytes 98312 | tf_op jit(solution)/shard_map/ppermute | solution.py:47
  66.0 4.6 %collective-permute-start.12 = (f32[64,128]{1,0:T(8,128)S(1)}, f32[64,128]{1,0:T(8,128)S(1)}, u32[]{:S(2)}, u32[]{:S(2)}) collective-permute-start(f32[64,128]{1,0:T(8,128)S(1)} %shard_map.84), channel_id=1, source_target_pairs={{0,2},{2,0},{4,6},{6,4},{1,3},{3,1},{5,7},{7,5},{8,10},{10,8},{12,... | collective-permute-start | bytes 98312 | tf_op jit(solution)/shard_map/ppermute | solution.py:47

commit v3 on v2

--- a/solution.py
+++ b/solution.py
@@ -22,11 +22,10 @@
 TILE = 128
 PANEL = 16
 NB = KB // TILE
-PAIRS = [(i, j) for i in range(NB) for j in range(i, NB)]
-HALF = len(PAIRS) // 2
 NY = 4
 NZ = 8
-CHUNK = HALF * TILE // NY
+SIDES = [(0, 1), (0, 2), (0, 3)], [(1, 2), (1, 3), (2, 3)]
+CHUNK = TILE + 8
 HIGH = lax.Precision.HIGHEST
 VMEM_LIMIT = 48 << 20
 VMEM_WHOLE = 40 << 20
@@ -217,13 +216,22 @@
 def gram_kernel(own_ref, other_ref, keep_ref, first_ref, second_ref, third_ref, half):
     rep = lax.axis_index("reps")
     y = lax.axis_index("examples") // NZ
-    for place in range(HALF):
-        low, high = PAIRS[place], PAIRS[HALF + place]
+
+    def product(low, high):
         row = pl.multiple_of(jnp.where(rep == 0, low[0], high[0]) * TILE, TILE)
         col = pl.multiple_of(jnp.where(rep == 0, low[1], high[1]) * TILE, TILE)
         total = dot(own_ref[:, pl.ds(row, TILE)], own_ref[:, pl.ds(col, TILE)], (0, 0))
         total += dot(other_ref[:, pl.ds(row, TILE)], other_ref[:, pl.ds(col, TILE)], (0, 0))
-        half[place * TILE : (place + 1) * TILE, :] = total * (1.0 / EXAMPLES)
+        return total * (1.0 / EXAMPLES)
+
+    row = lax.broadcasted_iota(jnp.int32, (TILE, TILE), 0)
+    col = lax.broadcasted_iota(jnp.int32, (TILE, TILE), 1)
+    upper, lower = product((0, 0), (2, 2)), product((1, 1), (3, 3))
+    half[...] = jnp.zeros_like(half)
+    half[:TILE, :] = jnp.where(row <= col, upper, lower)
+    half[TILE : TILE + 1, :] = jnp.sum(jnp.where(row == col, lower, 0.0), 0, keepdims=True)
+    for place, (low, high) in enumerate(zip(*SIDES), 1):
+        half[place * CHUNK : place * CHUNK + TILE, :] = product(low, high)
     for step, out_ref in enumerate((keep_ref, first_ref, second_ref, third_ref)):
         start = pl.multiple_of(lax.rem(y + step, NY) * CHUNK, 8)
         out_ref[...] = half[pl.ds(start, CHUNK), :]
@@ -283,20 +291,18 @@
     return jnp.concatenate(rows, 0)
 
 
-def solve_kernel(own_ref, other_ref, feats_ref, out_ref, gram, query):
+def solve_kernel(*refs):
+    pieces, (feats_ref, out_ref, gram, query) = refs[: 2 * NY], refs[2 * NY :]
     rep = lax.axis_index("reps")
     spot = lax.axis_index("examples")
     y, z = spot // NZ, lax.rem(spot, NZ)
-    piece = own_ref.shape[0] // NY
-    query_rows = piece - CHUNK
-    for side, ref in enumerate((own_ref, other_ref)):
-        holder = rep if side == 0 else 1 - rep
-        for step in range(NY):
-            source = lax.rem(y + NY - step, NY)
-            start = pl.multiple_of(holder * (HALF * TILE) + source * CHUNK, 8)
-            gram[pl.ds(start, CHUNK), :] = ref[step * piece : step * piece + CHUNK, :]
-            at = (side * NY + step) * query_rows
-            query[at : at + query_rows, :] = ref[step * piece + CHUNK : (step + 1) * piece, :]
+    query_rows = pieces[0].shape[0] - CHUNK
+    for place, ref in enumerate(pieces):
+        holder = rep if place < NY else 1 - rep
+        source = lax.rem(y + NY - place % NY, NY)
+        start = pl.multiple_of((holder * NY + source) * CHUNK, 8)
+        gram[pl.ds(start, CHUNK), :] = ref[:CHUNK, :]
+        query[place * query_rows : (place + 1) * query_rows, :] = ref[CHUNK:, :]
 
     total_rows = 2 * NY * query_rows
     r = lax.broadcasted_iota(jnp.int32, (total_rows, TILE), 0)
@@ -318,14 +324,22 @@
             for piece in split(query[...])
         )
 
-    eye = (
-        lax.broadcasted_iota(jnp.int32, (TILE, TILE), 0)
-        == lax.broadcasted_iota(jnp.int32, (TILE, TILE), 1)
-    ).astype(jnp.float32) * RIDGE
+    row = lax.broadcasted_iota(jnp.int32, (TILE, TILE), 0)
+    col = lax.broadcasted_iota(jnp.int32, (TILE, TILE), 1)
+    ridge = jnp.where(row == col, RIDGE, 0.0)
     block = {}
-    for place, (i, j) in enumerate(PAIRS):
-        value = gram[place * TILE : (place + 1) * TILE, :]
-        block[i, j] = value + eye if i == j else value
+    for core, pairs in enumerate(SIDES):
+        first = core * NY * CHUNK
+        packed = gram[first : first + TILE, :]
+        above = jnp.where(row < col, packed, 0.0)
+        block[2 * core, 2 * core] = jnp.where(row <= col, packed, above.T) + ridge
+        below = jnp.where(row > col, packed, 0.0)
+        diagonal = gram[first + TILE : first + TILE + 1, :]
+        other = jnp.where(row > col, packed, jnp.where(row == col, diagonal, below.T))
+        block[2 * core + 1, 2 * core + 1] = other + ridge
+        for place, pair in enumerate(pairs, 1):
+            start = first + place * CHUNK
+            block[pair] = gram[start : start + TILE, :]
 
     solved = []
     pending = [lambda c=c: pick(c) for c in range(NB)]
@@ -399,7 +413,7 @@
     keep, first, second, third = pl.pallas_call(
         gram_kernel,
         out_shape=[piece] * NY,
-        scratch_shapes=[pltpu.VMEM((HALF * TILE, TILE), jnp.float32)],
+        scratch_shapes=[pltpu.VMEM((NY * CHUNK, TILE), jnp.float32)],
         compiler_params=params,
     )(train_feats, other_feats)
     second = along_y(second, 2)
@@ -417,17 +431,17 @@
     second = along_y(held, 2)
     first = along_y(held, 1)
     third = along_y(held, 3)
-    mine = jnp.concatenate([held, first, second, third], 0)
-    theirs = move(mine, "reps", lambda r: 1 - r)
+    mine = [held, first, second, third]
+    theirs = [move(piece, "reps", lambda r: 1 - r) for piece in mine]
     value = pl.pallas_call(
         solve_kernel,
         out_shape=jax.ShapeDtypeStruct((train_feats.shape[0], TILE), jnp.float32),
         scratch_shapes=[
-            pltpu.VMEM((len(PAIRS) * TILE, TILE), jnp.float32),
+            pltpu.VMEM((2 * NY * CHUNK, TILE), jnp.float32),
             pltpu.VMEM((KB, TILE), jnp.float32),
         ],
         compiler_params=params,
-    )(mine, theirs, train_feats)
+    )(*mine, *theirs, train_feats)
     second = move(value, "shard", lambda s: s ^ 2)
     first = move(value, "shard", lambda s: s ^ 1)
     third = move(value, "shard", lambda s: s ^ 3)

time: 71.4 us -> 70.5 us (0.987)
  starting transfers between devices: 25.3 us -> 24.4 us
    ppermute x15 -> x18, starting transfers between devices: 25.3 us -> 24.4 us  [move(): return lax.ppermute(block, axis, [(i, target(i)) for i in range(count)])]
    ppermute x15 -> x18, waiting for transfers between devices: 24.1 us -> 24.1 us  [move(): return lax.ppermute(block, axis, [(i, target(i)) for i in range(count)])]
  transfers between devices with their start and end apart: 15 -> 18, of which waited for: 11 -> 14; matrix products, arithmetic and copies ran while one was open for 0% -> 0% of each run, Pallas kernels for 0% -> 0%
where the time goes in v3:
time: 70.5 us; the launch traced here: 70.4 us
  starting transfers between devices  24.4 us (35%)
  waiting for transfers between devices  24.1 us (34%)
  Pallas kernels  21 us (30%)
    ppermute x18, starting transfers between devices, move(): return lax.ppermute(block, axis, [(i, target(i)) for i in range(count)])  24.4 us
    ppermute x18, waiting for transfers between devices, move(): return lax.ppermute(block, axis, [(i, target(i)) for i in range(count)])  24.1 us
    pallas_call x1, Pallas kernels, on_device(): pl.pallas_call(solve_kernel, out_shape=jax.ShapeDtypeStruct((train_feats....  13.8 us
    pallas_call x1, Pallas kernels, features(): pl.pallas_call(feature_kernel, in_specs=[pl.BlockSpec(memory_space=pltpu....  6.41 us
  transfers between devices with their start and end apart: 18, of which 14 were waited for; matrix products, arithmetic and copies ran while one was open for 0% of the time, Pallas kernels for 0%

profile of v3, /device:TPU:32, one launch (start us, length us, event | category | flops | bytes accessed | tf_op | source)
XLA Modules:
  0.0 70.4 jit_solution(4655219683608412828)
XLA Ops:
  0.0 6.4 %shard_map.82 = (f32[64,512]{1,0:T(8,128)S(1)}, f32[8,128]{1,0:T(8,128)S(1)}) custom-call(s32[1,128]{1,0:T(1,128)} %bitcast.14, s32[1,128]{1,0:T(1,128)} %bitcast.15, bf16[32,16,128]{2,1,0:T(8,128)(2,1)} %bitcast.10, bf16[16,3584]{1,0:T(8,128)(2,1)} %bitcast.12, bf16[16,3584]{1,0:T(8,128)(2,1)} %bitcast.13, bf16[512,3584]{1,0:T(8,128)(2,1)} %bitcast.9, ...), custom_call_target="tpu_custom_call" | custom-call | tf_op jit(solution)/shard_map/pallas_call | solution.py:194
  6.5 1.3 %collective-permute-done.other_ref = f32[64,512]{1,0:T(8,128)S(1)} collective-permute-done((f32[64,512]{1,0:T(8,128)S(1)}, f32[64,512]{1,0:T(8,128)S(1)}, u32[]{:S(2)}, u32[]{:S(2)}) %collective-permute-start) | collective-permute-done | bytes 131104 | tf_op jit(solution)/shard_map/ppermute | solution.py:46
  7.9 0.8 %shard_map.83 = (f32[136,128]{1,0:T(8,128)S(1)}, f32[136,128]{1,0:T(8,128)S(1)}, f32[136,128]{1,0:T(8,128)S(1)}, f32[136,128]{1,0:T(8,128)S(1)}) custom-call(f32[64,512]{1,0:T(8,128)S(1)} %get-tuple-element.11.own_ref.refs_8_, f32[64,512]{1,0:T(8,128)S(1)} %collective-permute-done.other_ref), custom_call_target="tpu_custom_call" | custom-call | tf_op jit(solution)/shard_map/pallas_call | solution.py:413
  8.6 1.6 %collective-permute-start.1 = (f32[136,128]{1,0:T(8,128)S(1)}, f32[136,128]{1,0:T(8,128)S(1)}, u32[]{:S(2)}, u32[]{:S(2)}) collective-permute-start(f32[136,128]{1,0:T(8,128)S(1)} %get-tuple-element.13), channel_id=1, source_target_pairs={{0,64},{8,72},{16,80},{24,88},{32,96},{40,104},{48,112},{56,120},{... | collective-permute-start | bytes 208904 | tf_op jit(solution)/shard_map/ppermute | solution.py:46
  10.3 2.9 %collective-permute-start.2 = (f32[136,128]{1,0:T(8,128)S(1)}, f32[136,128]{1,0:T(8,128)S(1)}, u32[]{:S(2)}, u32[]{:S(2)}) collective-permute-start(f32[136,128]{1,0:T(8,128)S(1)} %get-tuple-element.14), channel_id=1, source_target_pairs={{0,128},{8,136},{16,144},{24,152},{32,160},{40,168},{48,176},{56,1... | collective-permute-start | bytes 208904 | tf_op jit(solution)/shard_map/ppermute | solution.py:46
  13.2 1.3 %collective-permute-start.3 = (f32[136,128]{1,0:T(8,128)S(1)}, f32[136,128]{1,0:T(8,128)S(1)}, u32[]{:S(2)}, u32[]{:S(2)}) collective-permute-start(f32[136,128]{1,0:T(8,128)S(1)} %get-tuple-element.15), channel_id=1, source_target_pairs={{0,192},{8,200},{16,208},{24,216},{32,224},{40,232},{48,240},{56,2... | collective-permute-start | bytes 208904 | tf_op jit(solution)/shard_map/ppermute | solution.py:46
  14.5 2.4 %collective-permute-done.2 = f32[136,128]{1,0:T(8,128)S(1)} collective-permute-done((f32[136,128]{1,0:T(8,128)S(1)}, f32[136,128]{1,0:T(8,128)S(1)}, u32[]{:S(2)}, u32[]{:S(2)}) %collective-permute-start.2) | collective-permute-done | bytes 69664 | tf_op jit(solution)/shard_map/ppermute | solution.py:46
  17.5 0.7 collective-permute-start.4
  18.2 3.8 %collective-permute-done.4 = f32[144,128]{1,0:T(8,128)S(1)} collective-permute-done((f32[144,128]{1,0:T(8,128)S(1)}, f32[144,128]{1,0:T(8,128)S(1)}, u32[]{:S(2)}, u32[]{:S(2)}) %collective-permute-start.4) | collective-permute-done | bytes 73760 | tf_op jit(solution)/shard_map/ppermute | solution.py:46
  22.0 6.9 %collective-permute-start.7 = (f32[152,128]{1,0:T(8,128)S(1)}, f32[152,128]{1,0:T(8,128)S(1)}, u32[]{:S(2)}, u32[]{:S(2)}) collective-permute-start(f32[152,128]{1,0:T(8,128)S(1)} %pad_maximum_fusion), channel_id=1, source_target_pairs={{0,32},{8,40},{16,48},{24,56},{32,0},{40,8},{48,16},{56,24},{64,96... | collective-permute-start | bytes 233480 | tf_op jit(solution)/shard_map/ppermute | solution.py:46
  28.9 2.9 %collective-permute-start.5 = (f32[152,128]{1,0:T(8,128)S(1)}, f32[152,128]{1,0:T(8,128)S(1)}, u32[]{:S(2)}, u32[]{:S(2)}) collective-permute-start(f32[152,128]{1,0:T(8,128)S(1)} %pad_maximum_fusion), channel_id=1, source_target_pairs={{0,16},{8,24},{16,32},{24,40},{32,48},{40,56},{48,0},{56,8},{64,80... | collective-permute-start | bytes 233480 | tf_op jit(solution)/shard_map/ppermute | solution.py:46
  32.1 2.2 %collective-permute-done.6 = f32[152,128]{1,0:T(8,128)S(1)} collective-permute-done((f32[152,128]{1,0:T(8,128)S(1)}, f32[152,128]{1,0:T(8,128)S(1)}, u32[]{:S(2)}, u32[]{:S(2)}) %collective-permute-start.6) | collective-permute-done | bytes 77856 | tf_op jit(solution)/shard_map/ppermute | solution.py:46
  34.3 2.0 %collective-permute-done.5 = f32[152,128]{1,0:T(8,128)S(1)} collective-permute-done((f32[152,128]{1,0:T(8,128)S(1)}, f32[152,128]{1,0:T(8,128)S(1)}, u32[]{:S(2)}, u32[]{:S(2)}) %collective-permute-start.5) | collective-permute-done | bytes 77856 | tf_op jit(solution)/shard_map/ppermute | solution.py:46
  36.4 2.8 %collective-permute-start.10 = (f32[200,128]{1,0:T(8,128)S(1)}, f32[200,128]{1,0:T(8,128)S(1)}, u32[]{:S(2)}, u32[]{:S(2)}) collective-permute-start(f32[200,128]{1,0:T(8,128)S(1)} %constant_dynamic-update-slice_fusion.refs_0_), channel_id=1, source_target_pairs={{0,192},{8,200},{16,208},{24,216},{32,224},{40,232},{48,240},{56,2... | collective-permute-start | bytes 307208 | tf_op jit(solution)/shard_map/ppermute | solution.py:46
  39.2 0.9 %collective-permute-start.8 = (f32[200,128]{1,0:T(8,128)S(1)}, f32[200,128]{1,0:T(8,128)S(1)}, u32[]{:S(2)}, u32[]{:S(2)}) collective-permute-start(f32[200,128]{1,0:T(8,128)S(1)} %constant_dynamic-update-slice_fusion.refs_0_), channel_id=1, source_target_pairs={{0,64},{8,72},{16,80},{24,88},{32,96},{40,104},{48,112},{56,120},{... | collective-permute-start | bytes 307208 | tf_op jit(solution)/shard_map/ppermute | solution.py:46
  40.1 2.3 %collective-permute-done.10.refs_3_ = f32[200,128]{1,0:T(8,128)S(1)} collective-permute-done((f32[200,128]{1,0:T(8,128)S(1)}, f32[200,128]{1,0:T(8,128)S(1)}, u32[]{:S(2)}, u32[]{:S(2)}) %collective-permute-start.10) | collective-permute-done | bytes 102432 | tf_op jit(solution)/shard_map/ppermute | solution.py:46
  42.5 3.0 %collective-permute-done.9.refs_2_ = f32[200,128]{1,0:T(8,128)S(1)} collective-permute-done((f32[200,128]{1,0:T(8,128)S(1)}, f32[200,128]{1,0:T(8,128)S(1)}, u32[]{:S(2)}, u32[]{:S(2)}) %collective-permute-start.9) | collective-permute-done | bytes 102432 | tf_op jit(solution)/shard_map/ppermute | solution.py:46
  45.4 0.8 %collective-permute-done.8.refs_1_ = f32[200,128]{1,0:T(8,128)S(1)} collective-permute-done((f32[200,128]{1,0:T(8,128)S(1)}, f32[200,128]{1,0:T(8,128)S(1)}, u32[]{:S(2)}, u32[]{:S(2)}) %collective-permute-start.8) | collective-permute-done | bytes 102432 | tf_op jit(solution)/shard_map/ppermute | solution.py:46
  46.7 0.8 %collective-permute-done.12.refs_5_ = f32[200,128]{1,0:T(8,128)S(1)} collective-permute-done((f32[200,128]{1,0:T(8,128)S(1)}, f32[200,128]{1,0:T(8,128)S(1)}, u32[]{:S(2)}, u32[]{:S(2)}) %collective-permute-start.12) | collective-permute-done | bytes 102432 | tf_op jit(solution)/shard_map/ppermute | solution.py:46
  47.5 13.8 %shard_map.84 = f32[64,128]{1,0:T(8,128)S(1)} custom-call(f32[200,128]{1,0:T(8,128)S(1)} %constant_dynamic-update-slice_fusion.refs_0_, f32[200,128]{1,0:T(8,128)S(1)} %collective-permute-done.8.refs_1_, f32[200,128]{1,0:T(8,128)S(1)} %collective-permute-done.9.refs_2_, f32[200,128]{1,0:T(8,128)S(1)} %collective-permute-done.10.refs_3_, ...), custom_call_target="tpu_custom_call" | custom-call | tf_op jit(solution)/shard_map/pallas_call | solution.py:436
  61.4 3.0 %collective-permute-start.17 = (f32[64,128]{1,0:T(8,128)S(1)}, f32[64,128]{1,0:T(8,128)S(1)}, u32[]{:S(2)}, u32[]{:S(2)}) collective-permute-start(f32[64,128]{1,0:T(8,128)S(1)} %shard_map.84), channel_id=1, source_target_pairs={{0,6},{2,4},{4,2},{6,0},{1,7},{3,5},{5,3},{7,1},{8,14},{10,12},{12... | collective-permute-start | bytes 98312 | tf_op jit(solution)/shard_map/ppermute | solution.py:46
  64.3 0.8 %collective-permute-start.16 = (f32[64,128]{1,0:T(8,128)S(1)}, f32[64,128]{1,0:T(8,128)S(1)}, u32[]{:S(2)}, u32[]{:S(2)}) collective-permute-start(f32[64,128]{1,0:T(8,128)S(1)} %shard_map.84), channel_id=1, source_target_pairs={{0,4},{2,6},{4,0},{6,2},{1,5},{3,7},{5,1},{7,3},{8,12},{10,14},{12... | collective-permute-start | bytes 98312 | tf_op jit(solution)/shard_map/ppermute | solution.py:46
  65.5 1.0 %collective-permute-done.17 = f32[64,128]{1,0:T(8,128)S(1)} collective-permute-done((f32[64,128]{1,0:T(8,128)S(1)}, f32[64,128]{1,0:T(8,128)S(1)}, u32[]{:S(2)}, u32[]{:S(2)}) %collective-permute-start.17) | collective-permute-done | bytes 32800 | tf_op jit(solution)/shard_map/ppermute | solution.py:46
  66.6 3.2 %collective-permute-done.16 = f32[64,128]{1,0:T(8,128)S(1)} collective-permute-done((f32[64,128]{1,0:T(8,128)S(1)}, f32[64,128]{1,0:T(8,128)S(1)}, u32[]{:S(2)}, u32[]{:S(2)}) %collective-permute-start.16) | collective-permute-done | bytes 32800 | tf_op jit(solution)/shard_map/ppermute | solution.py:46
  (27 shorter events, 2.8 us)
Async XLA Ops:
  6.4 1.4 %collective-permute-start = (f32[64,512]{1,0:T(8,128)S(1)}, f32[64,512]{1,0:T(8,128)S(1)}, u32[]{:S(2)}, u32[]{:S(2)}) collective-permute-start(f32[64,512]{1,0:T(8,128)S(1)} %get-tuple-element.11.own_ref.refs_8_), channel_id=1, source_target_pairs={{0,1},{1,0},{2,3},{3,2},{4,5},{5,4},{6,7},{7,6},{8,9},{9,8},{10,11... | collective-permute-start | bytes 393224 | tf_op jit(solution)/shard_map/ppermute | solution.py:46
  8.6 5.9 %collective-permute-start.1 = (f32[136,128]{1,0:T(8,128)S(1)}, f32[136,128]{1,0:T(8,128)S(1)}, u32[]{:S(2)}, u32[]{:S(2)}) collective-permute-start(f32[136,128]{1,0:T(8,128)S(1)} %get-tuple-element.13), channel_id=1, source_target_pairs={{0,64},{8,72},{16,80},{24,88},{32,96},{40,104},{48,112},{56,120},{... | collective-permute-start | bytes 208904 | tf_op jit(solution)/shard_map/ppermute | solution.py:46
  10.3 6.6 %collective-permute-start.2 = (f32[136,128]{1,0:T(8,128)S(1)}, f32[136,128]{1,0:T(8,128)S(1)}, u32[]{:S(2)}, u32[]{:S(2)}) collective-permute-start(f32[136,128]{1,0:T(8,128)S(1)} %get-tuple-element.14), channel_id=1, source_target_pairs={{0,128},{8,136},{16,144},{24,152},{32,160},{40,168},{48,176},{56,1... | collective-permute-start | bytes 208904 | tf_op jit(solution)/shard_map/ppermute | solution.py:46
  13.2 4.3 %collective-permute-start.3 = (f32[136,128]{1,0:T(8,128)S(1)}, f32[136,128]{1,0:T(8,128)S(1)}, u32[]{:S(2)}, u32[]{:S(2)}) collective-permute-start(f32[136,128]{1,0:T(8,128)S(1)} %get-tuple-element.15), channel_id=1, source_target_pairs={{0,192},{8,200},{16,208},{24,216},{32,224},{40,232},{48,240},{56,2... | collective-permute-start | bytes 208904 | tf_op jit(solution)/shard_map/ppermute | solution.py:46
  17.5 4.4 %collective-permute-start.4 = (f32[144,128]{1,0:T(8,128)S(1)}, f32[144,128]{1,0:T(8,128)S(1)}, u32[]{:S(2)}, u32[]{:S(2)}) collective-permute-start(f32[144,128]{1,0:T(8,128)S(1)} %pad_maximum_fusion.1), channel_id=1, source_target_pairs={{0,8},{8,0},{16,24},{24,16},{32,40},{40,32},{48,56},{56,48},{64,72... | collective-permute-start | bytes 221192 | tf_op jit(solution)/shard_map/ppermute | solution.py:46
  22.0 10.1 %collective-permute-start.7 = (f32[152,128]{1,0:T(8,128)S(1)}, f32[152,128]{1,0:T(8,128)S(1)}, u32[]{:S(2)}, u32[]{:S(2)}) collective-permute-start(f32[152,128]{1,0:T(8,128)S(1)} %pad_maximum_fusion), channel_id=1, source_target_pairs={{0,32},{8,40},{16,48},{24,56},{32,0},{40,8},{48,16},{56,24},{64,96... | collective-permute-start | bytes 233480 | tf_op jit(solution)/shard_map/ppermute | solution.py:46
  28.9 5.4 %collective-permute-start.6 = (f32[152,128]{1,0:T(8,128)S(1)}, f32[152,128]{1,0:T(8,128)S(1)}, u32[]{:S(2)}, u32[]{:S(2)}) collective-permute-start(f32[152,128]{1,0:T(8,128)S(1)} %pad_maximum_fusion), channel_id=1, source_target_pairs={{0,48},{8,56},{16,0},{24,8},{32,16},{40,24},{48,32},{56,40},{64,11... | collective-permute-start | bytes 233480 | tf_op jit(solution)/shard_map/ppermute | solution.py:46
  28.9 7.3 %collective-permute-start.5 = (f32[152,128]{1,0:T(8,128)S(1)}, f32[152,128]{1,0:T(8,128)S(1)}, u32[]{:S(2)}, u32[]{:S(2)}) collective-permute-start(f32[152,128]{1,0:T(8,128)S(1)} %pad_maximum_fusion), channel_id=1, source_target_pairs={{0,16},{8,24},{16,32},{24,40},{32,48},{40,56},{48,0},{56,8},{64,80... | collective-permute-start | bytes 233480 | tf_op jit(solution)/shard_map/ppermute | solution.py:46
  36.4 6.1 %collective-permute-start.10 = (f32[200,128]{1,0:T(8,128)S(1)}, f32[200,128]{1,0:T(8,128)S(1)}, u32[]{:S(2)}, u32[]{:S(2)}) collective-permute-start(f32[200,128]{1,0:T(8,128)S(1)} %constant_dynamic-update-slice_fusion.refs_0_), channel_id=1, source_target_pairs={{0,192},{8,200},{16,208},{24,216},{32,224},{40,232},{48,240},{56,2... | collective-permute-start | bytes 307208 | tf_op jit(solution)/shard_map/ppermute | solution.py:46
  39.1 6.3 %collective-permute-start.9 = (f32[200,128]{1,0:T(8,128)S(1)}, f32[200,128]{1,0:T(8,128)S(1)}, u32[]{:S(2)}, u32[]{:S(2)}) collective-permute-start(f32[200,128]{1,0:T(8,128)S(1)} %constant_dynamic-update-slice_fusion.refs_0_), channel_id=1, source_target_pairs={{0,128},{8,136},{16,144},{24,152},{32,160},{40,168},{48,176},{56,1... | collective-permute-start | bytes 307208 | tf_op jit(solution)/shard_map/ppermute | solution.py:46
  39.2 7.0 %collective-permute-start.8 = (f32[200,128]{1,0:T(8,128)S(1)}, f32[200,128]{1,0:T(8,128)S(1)}, u32[]{:S(2)}, u32[]{:S(2)}) collective-permute-start(f32[200,128]{1,0:T(8,128)S(1)} %constant_dynamic-update-slice_fusion.refs_0_), channel_id=1, source_target_pairs={{0,64},{8,72},{16,80},{24,88},{32,96},{40,104},{48,112},{56,120},{... | collective-permute-start | bytes 307208 | tf_op jit(solution)/shard_map/ppermute | solution.py:46
  40.1 6.1 %collective-permute-start.11 = (f32[200,128]{1,0:T(8,128)S(1)}, f32[200,128]{1,0:T(8,128)S(1)}, u32[]{:S(2)}, u32[]{:S(2)}) collective-permute-start(f32[200,128]{1,0:T(8,128)S(1)} %constant_dynamic-update-slice_fusion.refs_0_), channel_id=1, source_target_pairs={{0,1},{1,0},{2,3},{3,2},{4,5},{5,4},{6,7},{7,6},{8,9},{9,8},{10,11... | collective-permute-start | bytes 307208 | tf_op jit(solution)/shard_map/ppermute | solution.py:46
  42.4 3.8 %collective-permute-start.14 = (f32[200,128]{1,0:T(8,128)S(1)}, f32[200,128]{1,0:T(8,128)S(1)}, u32[]{:S(2)}, u32[]{:S(2)}) collective-permute-start(f32[200,128]{1,0:T(8,128)S(1)} %collective-permute-done.10.refs_3_), channel_id=1, source_target_pairs={{0,1},{1,0},{2,3},{3,2},{4,5},{5,4},{6,7},{7,6},{8,9},{9,8},{10,11... | collective-permute-start | bytes 307208 | tf_op jit(solution)/shard_map/ppermute | solution.py:46
  45.4 1.3 %collective-permute-start.13 = (f32[200,128]{1,0:T(8,128)S(1)}, f32[200,128]{1,0:T(8,128)S(1)}, u32[]{:S(2)}, u32[]{:S(2)}) collective-permute-start(f32[200,128]{1,0:T(8,128)S(1)} %collective-permute-done.9.refs_2_), channel_id=1, source_target_pairs={{0,1},{1,0},{2,3},{3,2},{4,5},{5,4},{6,7},{7,6},{8,9},{9,8},{10,11... | collective-permute-start | bytes 307208 | tf_op jit(solution)/shard_map/ppermute | solution.py:46
  46.2 1.3 %collective-permute-start.12 = (f32[200,128]{1,0:T(8,128)S(1)}, f32[200,128]{1,0:T(8,128)S(1)}, u32[]{:S(2)}, u32[]{:S(2)}) collective-permute-start(f32[200,128]{1,0:T(8,128)S(1)} %collective-permute-done.8.refs_1_), channel_id=1, source_target_pairs={{0,1},{1,0},{2,3},{3,2},{4,5},{5,4},{6,7},{7,6},{8,9},{9,8},{10,11... | collective-permute-start | bytes 307208 | tf_op jit(solution)/shard_map/ppermute | solution.py:46
  61.4 5.2 %collective-permute-start.17 = (f32[64,128]{1,0:T(8,128)S(1)}, f32[64,128]{1,0:T(8,128)S(1)}, u32[]{:S(2)}, u32[]{:S(2)}) collective-permute-start(f32[64,128]{1,0:T(8,128)S(1)} %shard_map.84), channel_id=1, source_target_pairs={{0,6},{2,4},{4,2},{6,0},{1,7},{3,5},{5,3},{7,1},{8,14},{10,12},{12... | collective-permute-start | bytes 98312 | tf_op jit(solution)/shard_map/ppermute | solution.py:46
  64.3 5.4 %collective-permute-start.16 = (f32[64,128]{1,0:T(8,128)S(1)}, f32[64,128]{1,0:T(8,128)S(1)}, u32[]{:S(2)}, u32[]{:S(2)}) collective-permute-start(f32[64,128]{1,0:T(8,128)S(1)} %shard_map.84), channel_id=1, source_target_pairs={{0,4},{2,6},{4,0},{6,2},{1,5},{3,7},{5,1},{7,3},{8,12},{10,14},{12... | collective-permute-start | bytes 98312 | tf_op jit(solution)/shard_map/ppermute | solution.py:46
  65.1 4.6 %collective-permute-start.15 = (f32[64,128]{1,0:T(8,128)S(1)}, f32[64,128]{1,0:T(8,128)S(1)}, u32[]{:S(2)}, u32[]{:S(2)}) collective-permute-start(f32[64,128]{1,0:T(8,128)S(1)} %shard_map.84), channel_id=1, source_target_pairs={{0,2},{2,0},{4,6},{6,4},{1,3},{3,1},{5,7},{7,5},{8,10},{10,8},{12,... | collective-permute-start | bytes 98312 | tf_op jit(solution)/shard_map/ppermute | solution.py:46

commit v4 on v3

--- a/solution.py
+++ b/solution.py
@@ -39,6 +39,13 @@
         precision=HIGH,
         preferred_element_type=jnp.float32,
     )
+
+
+def short_dot(a, b):
+    a_high, a_low, _ = split(a)
+    b_high, b_low, _ = split(b)
+    terms = ((a_low, b_high), (a_high, b_low), (a_high, b_high))
+    return sum(jnp.dot(x, y, preferred_element_type=jnp.float32) for x, y in terms)
 
 
 def move(block, axis, target):
@@ -382,9 +389,9 @@
         value = solved[b][NB - 1 - b]
         if b < NB - 1:
             later = jnp.concatenate(answer[b + 1 :], 0)
-            value = value - dot(jnp.concatenate(solved[b][: NB - 1 - b], 1), later)
+            value = value - short_dot(jnp.concatenate(solved[b][: NB - 1 - b], 1), later)
         answer[b] = value
-    out_ref[...] = dot(feats_ref[...], jnp.concatenate(answer, 0)) * (1.0 / math.sqrt(4 * KB))
+    out_ref[...] = short_dot(feats_ref[...], jnp.concatenate(answer, 0)) * (1.0 / math.sqrt(4 * KB))
 
 
 def on_device(

time: 70.5 us -> 70.1 us (level)
  no operation moved by 1% of the time
where the time goes in v4:
time: 70.1 us
  starting transfers between devices  24.4 us (35%)
  waiting for transfers between devices  24.1 us (34%)
  Pallas kernels  20.7 us (30%)
    ppermute x18, starting transfers between devices, move(): return lax.ppermute(block, axis, [(i, target(i)) for i in range(count)])  24.4 us
    ppermute x18, waiting for transfers between devices, move(): return lax.ppermute(block, axis, [(i, target(i)) for i in range(count)])  24.1 us
    pallas_call x1, Pallas kernels, on_device(): pl.pallas_call(solve_kernel, out_shape=jax.ShapeDtypeStruct((train_feats....  13.5 us
    pallas_call x1, Pallas kernels, features(): pl.pallas_call(feature_kernel, in_specs=[pl.BlockSpec(memory_space=pltpu....  6.41 us
  transfers between devices with their start and end apart: 18, of which 14 were waited for; matrix products, arithmetic and copies ran while one was open for 0% of the time, Pallas kernels for 0%

profile of v4, /device:TPU:32, one launch (start us, length us, event | category | flops | bytes accessed | tf_op | source)
XLA Modules:
  0.0 70.1 jit_solution(17405437657249900628)
XLA Ops:
  0.0 6.4 %shard_map.82 = (f32[64,512]{1,0:T(8,128)S(1)}, f32[8,128]{1,0:T(8,128)S(1)}) custom-call(s32[1,128]{1,0:T(1,128)} %bitcast.14, s32[1,128]{1,0:T(1,128)} %bitcast.15, bf16[32,16,128]{2,1,0:T(8,128)(2,1)} %bitcast.10, bf16[16,3584]{1,0:T(8,128)(2,1)} %bitcast.12, bf16[16,3584]{1,0:T(8,128)(2,1)} %bitcast.13, bf16[512,3584]{1,0:T(8,128)(2,1)} %bitcast.9, ...), custom_call_target="tpu_custom_call" | custom-call | tf_op jit(solution)/shard_map/pallas_call | solution.py:201
  6.5 1.3 %collective-permute-done.other_ref = f32[64,512]{1,0:T(8,128)S(1)} collective-permute-done((f32[64,512]{1,0:T(8,128)S(1)}, f32[64,512]{1,0:T(8,128)S(1)}, u32[]{:S(2)}, u32[]{:S(2)}) %collective-permute-start) | collective-permute-done | bytes 131104 | tf_op jit(solution)/shard_map/ppermute | solution.py:53
  7.9 0.8 %shard_map.83 = (f32[136,128]{1,0:T(8,128)S(1)}, f32[136,128]{1,0:T(8,128)S(1)}, f32[136,128]{1,0:T(8,128)S(1)}, f32[136,128]{1,0:T(8,128)S(1)}) custom-call(f32[64,512]{1,0:T(8,128)S(1)} %get-tuple-element.11.own_ref.refs_8_, f32[64,512]{1,0:T(8,128)S(1)} %collective-permute-done.other_ref), custom_call_target="tpu_custom_call" | custom-call | tf_op jit(solution)/shard_map/pallas_call | solution.py:420
  8.6 1.6 %collective-permute-start.1 = (f32[136,128]{1,0:T(8,128)S(1)}, f32[136,128]{1,0:T(8,128)S(1)}, u32[]{:S(2)}, u32[]{:S(2)}) collective-permute-start(f32[136,128]{1,0:T(8,128)S(1)} %get-tuple-element.13), channel_id=1, source_target_pairs={{0,64},{8,72},{16,80},{24,88},{32,96},{40,104},{48,112},{56,120},{... | collective-permute-start | bytes 208904 | tf_op jit(solution)/shard_map/ppermute | solution.py:53
  10.3 2.9 %collective-permute-start.2 = (f32[136,128]{1,0:T(8,128)S(1)}, f32[136,128]{1,0:T(8,128)S(1)}, u32[]{:S(2)}, u32[]{:S(2)}) collective-permute-start(f32[136,128]{1,0:T(8,128)S(1)} %get-tuple-element.14), channel_id=1, source_target_pairs={{0,128},{8,136},{16,144},{24,152},{32,160},{40,168},{48,176},{56,1... | collective-permute-start | bytes 208904 | tf_op jit(solution)/shard_map/ppermute | solution.py:53
  13.2 1.3 %collective-permute-start.3 = (f32[136,128]{1,0:T(8,128)S(1)}, f32[136,128]{1,0:T(8,128)S(1)}, u32[]{:S(2)}, u32[]{:S(2)}) collective-permute-start(f32[136,128]{1,0:T(8,128)S(1)} %get-tuple-element.15), channel_id=1, source_target_pairs={{0,192},{8,200},{16,208},{24,216},{32,224},{40,232},{48,240},{56,2... | collective-permute-start | bytes 208904 | tf_op jit(solution)/shard_map/ppermute | solution.py:53
  14.5 2.4 %collective-permute-done.2 = f32[136,128]{1,0:T(8,128)S(1)} collective-permute-done((f32[136,128]{1,0:T(8,128)S(1)}, f32[136,128]{1,0:T(8,128)S(1)}, u32[]{:S(2)}, u32[]{:S(2)}) %collective-permute-start.2) | collective-permute-done | bytes 69664 | tf_op jit(solution)/shard_map/ppermute | solution.py:53
  17.5 0.7 collective-permute-start.4
  18.2 3.8 %collective-permute-done.4 = f32[144,128]{1,0:T(8,128)S(1)} collective-permute-done((f32[144,128]{1,0:T(8,128)S(1)}, f32[144,128]{1,0:T(8,128)S(1)}, u32[]{:S(2)}, u32[]{:S(2)}) %collective-permute-start.4) | collective-permute-done | bytes 73760 | tf_op jit(solution)/shard_map/ppermute | solution.py:53
  22.0 6.9 %collective-permute-start.7 = (f32[152,128]{1,0:T(8,128)S(1)}, f32[152,128]{1,0:T(8,128)S(1)}, u32[]{:S(2)}, u32[]{:S(2)}) collective-permute-start(f32[152,128]{1,0:T(8,128)S(1)} %pad_maximum_fusion), channel_id=1, source_target_pairs={{0,32},{8,40},{16,48},{24,56},{32,0},{40,8},{48,16},{56,24},{64,96... | collective-permute-start | bytes 233480 | tf_op jit(solution)/shard_map/ppermute | solution.py:53
  28.9 2.9 %collective-permute-start.5 = (f32[152,128]{1,0:T(8,128)S(1)}, f32[152,128]{1,0:T(8,128)S(1)}, u32[]{:S(2)}, u32[]{:S(2)}) collective-permute-start(f32[152,128]{1,0:T(8,128)S(1)} %pad_maximum_fusion), channel_id=1, source_target_pairs={{0,16},{8,24},{16,32},{24,40},{32,48},{40,56},{48,0},{56,8},{64,80... | collective-permute-start | bytes 233480 | tf_op jit(solution)/shard_map/ppermute | solution.py:53
  32.1 2.2 %collective-permute-done.6 = f32[152,128]{1,0:T(8,128)S(1)} collective-permute-done((f32[152,128]{1,0:T(8,128)S(1)}, f32[152,128]{1,0:T(8,128)S(1)}, u32[]{:S(2)}, u32[]{:S(2)}) %collective-permute-start.6) | collective-permute-done | bytes 77856 | tf_op jit(solution)/shard_map/ppermute | solution.py:53
  34.3 2.0 %collective-permute-done.5 = f32[152,128]{1,0:T(8,128)S(1)} collective-permute-done((f32[152,128]{1,0:T(8,128)S(1)}, f32[152,128]{1,0:T(8,128)S(1)}, u32[]{:S(2)}, u32[]{:S(2)}) %collective-permute-start.5) | collective-permute-done | bytes 77856 | tf_op jit(solution)/shard_map/ppermute | solution.py:53
  36.4 2.8 %collective-permute-start.10 = (f32[200,128]{1,0:T(8,128)S(1)}, f32[200,128]{1,0:T(8,128)S(1)}, u32[]{:S(2)}, u32[]{:S(2)}) collective-permute-start(f32[200,128]{1,0:T(8,128)S(1)} %constant_dynamic-update-slice_fusion.refs_0_), channel_id=1, source_target_pairs={{0,192},{8,200},{16,208},{24,216},{32,224},{40,232},{48,240},{56,2... | collective-permute-start | bytes 307208 | tf_op jit(solution)/shard_map/ppermute | solution.py:53
  39.2 0.9 %collective-permute-start.8 = (f32[200,128]{1,0:T(8,128)S(1)}, f32[200,128]{1,0:T(8,128)S(1)}, u32[]{:S(2)}, u32[]{:S(2)}) collective-permute-start(f32[200,128]{1,0:T(8,128)S(1)} %constant_dynamic-update-slice_fusion.refs_0_), channel_id=1, source_target_pairs={{0,64},{8,72},{16,80},{24,88},{32,96},{40,104},{48,112},{56,120},{... | collective-permute-start | bytes 307208 | tf_op jit(solution)/shard_map/ppermute | solution.py:53
  40.1 2.3 %collective-permute-done.10.refs_3_ = f32[200,128]{1,0:T(8,128)S(1)} collective-permute-done((f32[200,128]{1,0:T(8,128)S(1)}, f32[200,128]{1,0:T(8,128)S(1)}, u32[]{:S(2)}, u32[]{:S(2)}) %collective-permute-start.10) | collective-permute-done | bytes 102432 | tf_op jit(solution)/shard_map/ppermute | solution.py:53
  42.5 3.0 %collective-permute-done.9.refs_2_ = f32[200,128]{1,0:T(8,128)S(1)} collective-permute-done((f32[200,128]{1,0:T(8,128)S(1)}, f32[200,128]{1,0:T(8,128)S(1)}, u32[]{:S(2)}, u32[]{:S(2)}) %collective-permute-start.9) | collective-permute-done | bytes 102432 | tf_op jit(solution)/shard_map/ppermute | solution.py:53
  45.4 0.8 %collective-permute-done.8.refs_1_ = f32[200,128]{1,0:T(8,128)S(1)} collective-permute-done((f32[200,128]{1,0:T(8,128)S(1)}, f32[200,128]{1,0:T(8,128)S(1)}, u32[]{:S(2)}, u32[]{:S(2)}) %collective-permute-start.8) | collective-permute-done | bytes 102432 | tf_op jit(solution)/shard_map/ppermute | solution.py:53
  46.7 0.8 %collective-permute-done.12.refs_5_ = f32[200,128]{1,0:T(8,128)S(1)} collective-permute-done((f32[200,128]{1,0:T(8,128)S(1)}, f32[200,128]{1,0:T(8,128)S(1)}, u32[]{:S(2)}, u32[]{:S(2)}) %collective-permute-start.12) | collective-permute-done | bytes 102432 | tf_op jit(solution)/shard_map/ppermute | solution.py:53
  47.5 13.5 %shard_map.84 = f32[64,128]{1,0:T(8,128)S(1)} custom-call(f32[200,128]{1,0:T(8,128)S(1)} %constant_dynamic-update-slice_fusion.refs_0_, f32[200,128]{1,0:T(8,128)S(1)} %collective-permute-done.8.refs_1_, f32[200,128]{1,0:T(8,128)S(1)} %collective-permute-done.9.refs_2_, f32[200,128]{1,0:T(8,128)S(1)} %collective-permute-done.10.refs_3_, ...), custom_call_target="tpu_custom_call" | custom-call | tf_op jit(solution)/shard_map/pallas_call | solution.py:443
  61.0 3.0 %collective-permute-start.17 = (f32[64,128]{1,0:T(8,128)S(1)}, f32[64,128]{1,0:T(8,128)S(1)}, u32[]{:S(2)}, u32[]{:S(2)}) collective-permute-start(f32[64,128]{1,0:T(8,128)S(1)} %shard_map.84), channel_id=1, source_target_pairs={{0,6},{2,4},{4,2},{6,0},{1,7},{3,5},{5,3},{7,1},{8,14},{10,12},{12... | collective-permute-start | bytes 98312 | tf_op jit(solution)/shard_map/ppermute | solution.py:53
  64.0 0.8 %collective-permute-start.16 = (f32[64,128]{1,0:T(8,128)S(1)}, f32[64,128]{1,0:T(8,128)S(1)}, u32[]{:S(2)}, u32[]{:S(2)}) collective-permute-start(f32[64,128]{1,0:T(8,128)S(1)} %shard_map.84), channel_id=1, source_target_pairs={{0,4},{2,6},{4,0},{6,2},{1,5},{3,7},{5,1},{7,3},{8,12},{10,14},{12... | collective-permute-start | bytes 98312 | tf_op jit(solution)/shard_map/ppermute | solution.py:53
  65.2 1.0 %collective-permute-done.17 = f32[64,128]{1,0:T(8,128)S(1)} collective-permute-done((f32[64,128]{1,0:T(8,128)S(1)}, f32[64,128]{1,0:T(8,128)S(1)}, u32[]{:S(2)}, u32[]{:S(2)}) %collective-permute-start.17) | collective-permute-done | bytes 32800 | tf_op jit(solution)/shard_map/ppermute | solution.py:53
  66.2 3.2 %collective-permute-done.16 = f32[64,128]{1,0:T(8,128)S(1)} collective-permute-done((f32[64,128]{1,0:T(8,128)S(1)}, f32[64,128]{1,0:T(8,128)S(1)}, u32[]{:S(2)}, u32[]{:S(2)}) %collective-permute-start.16) | collective-permute-done | bytes 32800 | tf_op jit(solution)/shard_map/ppermute | solution.py:53
  (27 shorter events, 2.8 us)
Async XLA Ops:
  6.4 1.4 %collective-permute-start = (f32[64,512]{1,0:T(8,128)S(1)}, f32[64,512]{1,0:T(8,128)S(1)}, u32[]{:S(2)}, u32[]{:S(2)}) collective-permute-start(f32[64,512]{1,0:T(8,128)S(1)} %get-tuple-element.11.own_ref.refs_8_), channel_id=1, source_target_pairs={{0,1},{1,0},{2,3},{3,2},{4,5},{5,4},{6,7},{7,6},{8,9},{9,8},{10,11... | collective-permute-start | bytes 393224 | tf_op jit(solution)/shard_map/ppermute | solution.py:53
  8.6 5.9 %collective-permute-start.1 = (f32[136,128]{1,0:T(8,128)S(1)}, f32[136,128]{1,0:T(8,128)S(1)}, u32[]{:S(2)}, u32[]{:S(2)}) collective-permute-start(f32[136,128]{1,0:T(8,128)S(1)} %get-tuple-element.13), channel_id=1, source_target_pairs={{0,64},{8,72},{16,80},{24,88},{32,96},{40,104},{48,112},{56,120},{... | collective-permute-start | bytes 208904 | tf_op jit(solution)/shard_map/ppermute | solution.py:53
  10.3 6.6 %collective-permute-start.2 = (f32[136,128]{1,0:T(8,128)S(1)}, f32[136,128]{1,0:T(8,128)S(1)}, u32[]{:S(2)}, u32[]{:S(2)}) collective-permute-start(f32[136,128]{1,0:T(8,128)S(1)} %get-tuple-element.14), channel_id=1, source_target_pairs={{0,128},{8,136},{16,144},{24,152},{32,160},{40,168},{48,176},{56,1... | collective-permute-start | bytes 208904 | tf_op jit(solution)/shard_map/ppermute | solution.py:53
  13.2 4.3 %collective-permute-start.3 = (f32[136,128]{1,0:T(8,128)S(1)}, f32[136,128]{1,0:T(8,128)S(1)}, u32[]{:S(2)}, u32[]{:S(2)}) collective-permute-start(f32[136,128]{1,0:T(8,128)S(1)} %get-tuple-element.15), channel_id=1, source_target_pairs={{0,192},{8,200},{16,208},{24,216},{32,224},{40,232},{48,240},{56,2... | collective-permute-start | bytes 208904 | tf_op jit(solution)/shard_map/ppermute | solution.py:53
  17.5 4.4 %collective-permute-start.4 = (f32[144,128]{1,0:T(8,128)S(1)}, f32[144,128]{1,0:T(8,128)S(1)}, u32[]{:S(2)}, u32[]{:S(2)}) collective-permute-start(f32[144,128]{1,0:T(8,128)S(1)} %pad_maximum_fusion.1), channel_id=1, source_target_pairs={{0,8},{8,0},{16,24},{24,16},{32,40},{40,32},{48,56},{56,48},{64,72... | collective-permute-start | bytes 221192 | tf_op jit(solution)/shard_map/ppermute | solution.py:53
  22.0 10.1 %collective-permute-start.7 = (f32[152,128]{1,0:T(8,128)S(1)}, f32[152,128]{1,0:T(8,128)S(1)}, u32[]{:S(2)}, u32[]{:S(2)}) collective-permute-start(f32[152,128]{1,0:T(8,128)S(1)} %pad_maximum_fusion), channel_id=1, source_target_pairs={{0,32},{8,40},{16,48},{24,56},{32,0},{40,8},{48,16},{56,24},{64,96... | collective-permute-start | bytes 233480 | tf_op jit(solution)/shard_map/ppermute | solution.py:53
  28.9 5.4 %collective-permute-start.6 = (f32[152,128]{1,0:T(8,128)S(1)}, f32[152,128]{1,0:T(8,128)S(1)}, u32[]{:S(2)}, u32[]{:S(2)}) collective-permute-start(f32[152,128]{1,0:T(8,128)S(1)} %pad_maximum_fusion), channel_id=1, source_target_pairs={{0,48},{8,56},{16,0},{24,8},{32,16},{40,24},{48,32},{56,40},{64,11... | collective-permute-start | bytes 233480 | tf_op jit(solution)/shard_map/ppermute | solution.py:53
  28.9 7.3 %collective-permute-start.5 = (f32[152,128]{1,0:T(8,128)S(1)}, f32[152,128]{1,0:T(8,128)S(1)}, u32[]{:S(2)}, u32[]{:S(2)}) collective-permute-start(f32[152,128]{1,0:T(8,128)S(1)} %pad_maximum_fusion), channel_id=1, source_target_pairs={{0,16},{8,24},{16,32},{24,40},{32,48},{40,56},{48,0},{56,8},{64,80... | collective-permute-start | bytes 233480 | tf_op jit(solution)/shard_map/ppermute | solution.py:53
  36.4 6.1 %collective-permute-start.10 = (f32[200,128]{1,0:T(8,128)S(1)}, f32[200,128]{1,0:T(8,128)S(1)}, u32[]{:S(2)}, u32[]{:S(2)}) collective-permute-start(f32[200,128]{1,0:T(8,128)S(1)} %constant_dynamic-update-slice_fusion.refs_0_), channel_id=1, source_target_pairs={{0,192},{8,200},{16,208},{24,216},{32,224},{40,232},{48,240},{56,2... | collective-permute-start | bytes 307208 | tf_op jit(solution)/shard_map/ppermute | solution.py:53
  39.1 6.3 %collective-permute-start.9 = (f32[200,128]{1,0:T(8,128)S(1)}, f32[200,128]{1,0:T(8,128)S(1)}, u32[]{:S(2)}, u32[]{:S(2)}) collective-permute-start(f32[200,128]{1,0:T(8,128)S(1)} %constant_dynamic-update-slice_fusion.refs_0_), channel_id=1, source_target_pairs={{0,128},{8,136},{16,144},{24,152},{32,160},{40,168},{48,176},{56,1... | collective-permute-start | bytes 307208 | tf_op jit(solution)/shard_map/ppermute | solution.py:53
  39.2 7.0 %collective-permute-start.8 = (f32[200,128]{1,0:T(8,128)S(1)}, f32[200,128]{1,0:T(8,128)S(1)}, u32[]{:S(2)}, u32[]{:S(2)}) collective-permute-start(f32[200,128]{1,0:T(8,128)S(1)} %constant_dynamic-update-slice_fusion.refs_0_), channel_id=1, source_target_pairs={{0,64},{8,72},{16,80},{24,88},{32,96},{40,104},{48,112},{56,120},{... | collective-permute-start | bytes 307208 | tf_op jit(solution)/shard_map/ppermute | solution.py:53
  40.1 6.1 %collective-permute-start.11 = (f32[200,128]{1,0:T(8,128)S(1)}, f32[200,128]{1,0:T(8,128)S(1)}, u32[]{:S(2)}, u32[]{:S(2)}) collective-permute-start(f32[200,128]{1,0:T(8,128)S(1)} %constant_dynamic-update-slice_fusion.refs_0_), channel_id=1, source_target_pairs={{0,1},{1,0},{2,3},{3,2},{4,5},{5,4},{6,7},{7,6},{8,9},{9,8},{10,11... | collective-permute-start | bytes 307208 | tf_op jit(solution)/shard_map/ppermute | solution.py:53
  42.4 3.8 %collective-permute-start.14 = (f32[200,128]{1,0:T(8,128)S(1)}, f32[200,128]{1,0:T(8,128)S(1)}, u32[]{:S(2)}, u32[]{:S(2)}) collective-permute-start(f32[200,128]{1,0:T(8,128)S(1)} %collective-permute-done.10.refs_3_), channel_id=1, source_target_pairs={{0,1},{1,0},{2,3},{3,2},{4,5},{5,4},{6,7},{7,6},{8,9},{9,8},{10,11... | collective-permute-start | bytes 307208 | tf_op jit(solution)/shard_map/ppermute | solution.py:53
  45.4 1.3 %collective-permute-start.13 = (f32[200,128]{1,0:T(8,128)S(1)}, f32[200,128]{1,0:T(8,128)S(1)}, u32[]{:S(2)}, u32[]{:S(2)}) collective-permute-start(f32[200,128]{1,0:T(8,128)S(1)} %collective-permute-done.9.refs_2_), channel_id=1, source_target_pairs={{0,1},{1,0},{2,3},{3,2},{4,5},{5,4},{6,7},{7,6},{8,9},{9,8},{10,11... | collective-permute-start | bytes 307208 | tf_op jit(solution)/shard_map/ppermute | solution.py:53
  46.2 1.3 %collective-permute-start.12 = (f32[200,128]{1,0:T(8,128)S(1)}, f32[200,128]{1,0:T(8,128)S(1)}, u32[]{:S(2)}, u32[]{:S(2)}) collective-permute-start(f32[200,128]{1,0:T(8,128)S(1)} %collective-permute-done.8.refs_1_), channel_id=1, source_target_pairs={{0,1},{1,0},{2,3},{3,2},{4,5},{5,4},{6,7},{7,6},{8,9},{9,8},{10,11... | collective-permute-start | bytes 307208 | tf_op jit(solution)/shard_map/ppermute | solution.py:53
  61.0 5.2 %collective-permute-start.17 = (f32[64,128]{1,0:T(8,128)S(1)}, f32[64,128]{1,0:T(8,128)S(1)}, u32[]{:S(2)}, u32[]{:S(2)}) collective-permute-start(f32[64,128]{1,0:T(8,128)S(1)} %shard_map.84), channel_id=1, source_target_pairs={{0,6},{2,4},{4,2},{6,0},{1,7},{3,5},{5,3},{7,1},{8,14},{10,12},{12... | collective-permute-start | bytes 98312 | tf_op jit(solution)/shard_map/ppermute | solution.py:53
  64.0 5.4 %collective-permute-start.16 = (f32[64,128]{1,0:T(8,128)S(1)}, f32[64,128]{1,0:T(8,128)S(1)}, u32[]{:S(2)}, u32[]{:S(2)}) collective-permute-start(f32[64,128]{1,0:T(8,128)S(1)} %shard_map.84), channel_id=1, source_target_pairs={{0,4},{2,6},{4,0},{6,2},{1,5},{3,7},{5,1},{7,3},{8,12},{10,14},{12... | collective-permute-start | bytes 98312 | tf_op jit(solution)/shard_map/ppermute | solution.py:53
  64.8 4.6 %collective-permute-start.15 = (f32[64,128]{1,0:T(8,128)S(1)}, f32[64,128]{1,0:T(8,128)S(1)}, u32[]{:S(2)}, u32[]{:S(2)}) collective-permute-start(f32[64,128]{1,0:T(8,128)S(1)} %shard_map.84), channel_id=1, source_target_pairs={{0,2},{2,0},{4,6},{6,4},{1,3},{3,1},{5,7},{7,5},{8,10},{10,8},{12,... | collective-permute-start | bytes 98312 | tf_op jit(solution)/shard_map/ppermute | solution.py:53

commit v5 on v4

--- a/solution.py
+++ b/solution.py
@@ -355,7 +355,14 @@
         if pending:
             pending.pop(0)()
 
+    turned = {}
+
+    def turn(b):
+        turned[b] = block[b, b + 1].T
+
     for b in range(NB):
+        if b < NB - 1:
+            pending.append(lambda b=b: turn(b))
         inverse = block_inverse(block[b, b], between)
         while pending:
             between()
@@ -363,7 +370,7 @@
             solved.append([dot(inverse, right[b])])
             break
         near = dot(inverse, block[b, b + 1])
-        block[b + 1, b + 1] = block[b + 1, b + 1] - dot(block[b, b + 1], near, (0, 0))
+        block[b + 1, b + 1] = block[b + 1, b + 1] - dot(turned[b], near)
         done = [near]
         solved.append(done)
 

time: 70.1 us -> 70.1 us (level)
  no operation moved by 1% of the time
where the time goes in v5:
time: 70.1 us
  starting transfers between devices  24.4 us (35%)
  waiting for transfers between devices  24.1 us (34%)
  Pallas kernels  20.7 us (30%)
    ppermute x18, starting transfers between devices, move(): return lax.ppermute(block, axis, [(i, target(i)) for i in range(count)])  24.4 us
    ppermute x18, waiting for transfers between devices, move(): return lax.ppermute(block, axis, [(i, target(i)) for i in range(count)])  24.1 us
    pallas_call x1, Pallas kernels, on_device(): pl.pallas_call(solve_kernel, out_shape=jax.ShapeDtypeStruct((train_feats....  13.5 us
    pallas_call x1, Pallas kernels, features(): pl.pallas_call(feature_kernel, in_specs=[pl.BlockSpec(memory_space=pltpu....  6.41 us
  transfers between devices with their start and end apart: 18, of which 14 were waited for; matrix products, arithmetic and copies ran while one was open for 0% of the time, Pallas kernels for 0%

profile of v5, /device:TPU:32, one launch (start us, length us, event | category | flops | bytes accessed | tf_op | source)
XLA Modules:
  0.0 70.1 jit_solution(17405437657249900628)
XLA Ops:
  0.0 6.4 %shard_map.82 = (f32[64,512]{1,0:T(8,128)S(1)}, f32[8,128]{1,0:T(8,128)S(1)}) custom-call(s32[1,128]{1,0:T(1,128)} %bitcast.14, s32[1,128]{1,0:T(1,128)} %bitcast.15, bf16[32,16,128]{2,1,0:T(8,128)(2,1)} %bitcast.10, bf16[16,3584]{1,0:T(8,128)(2,1)} %bitcast.12, bf16[16,3584]{1,0:T(8,128)(2,1)} %bitcast.13, bf16[512,3584]{1,0:T(8,128)(2,1)} %bitcast.9, ...), custom_call_target="tpu_custom_call" | custom-call | tf_op jit(solution)/shard_map/pallas_call | solution.py:201
  6.5 1.3 %collective-permute-done.other_ref = f32[64,512]{1,0:T(8,128)S(1)} collective-permute-done((f32[64,512]{1,0:T(8,128)S(1)}, f32[64,512]{1,0:T(8,128)S(1)}, u32[]{:S(2)}, u32[]{:S(2)}) %collective-permute-start) | collective-permute-done | bytes 131104 | tf_op jit(solution)/shard_map/ppermute | solution.py:53
  7.9 0.8 %shard_map.83 = (f32[136,128]{1,0:T(8,128)S(1)}, f32[136,128]{1,0:T(8,128)S(1)}, f32[136,128]{1,0:T(8,128)S(1)}, f32[136,128]{1,0:T(8,128)S(1)}) custom-call(f32[64,512]{1,0:T(8,128)S(1)} %get-tuple-element.11.own_ref.refs_8_, f32[64,512]{1,0:T(8,128)S(1)} %collective-permute-done.other_ref), custom_call_target="tpu_custom_call" | custom-call | tf_op jit(solution)/shard_map/pallas_call | solution.py:427
  8.6 1.6 %collective-permute-start.1 = (f32[136,128]{1,0:T(8,128)S(1)}, f32[136,128]{1,0:T(8,128)S(1)}, u32[]{:S(2)}, u32[]{:S(2)}) collective-permute-start(f32[136,128]{1,0:T(8,128)S(1)} %get-tuple-element.13), channel_id=1, source_target_pairs={{0,64},{8,72},{16,80},{24,88},{32,96},{40,104},{48,112},{56,120},{... | collective-permute-start | bytes 208904 | tf_op jit(solution)/shard_map/ppermute | solution.py:53
  10.3 2.9 %collective-permute-start.2 = (f32[136,128]{1,0:T(8,128)S(1)}, f32[136,128]{1,0:T(8,128)S(1)}, u32[]{:S(2)}, u32[]{:S(2)}) collective-permute-start(f32[136,128]{1,0:T(8,128)S(1)} %get-tuple-element.14), channel_id=1, source_target_pairs={{0,128},{8,136},{16,144},{24,152},{32,160},{40,168},{48,176},{56,1... | collective-permute-start | bytes 208904 | tf_op jit(solution)/shard_map/ppermute | solution.py:53
  13.2 1.3 %collective-permute-start.3 = (f32[136,128]{1,0:T(8,128)S(1)}, f32[136,128]{1,0:T(8,128)S(1)}, u32[]{:S(2)}, u32[]{:S(2)}) collective-permute-start(f32[136,128]{1,0:T(8,128)S(1)} %get-tuple-element.15), channel_id=1, source_target_pairs={{0,192},{8,200},{16,208},{24,216},{32,224},{40,232},{48,240},{56,2... | collective-permute-start | bytes 208904 | tf_op jit(solution)/shard_map/ppermute | solution.py:53
  14.5 2.4 %collective-permute-done.2 = f32[136,128]{1,0:T(8,128)S(1)} collective-permute-done((f32[136,128]{1,0:T(8,128)S(1)}, f32[136,128]{1,0:T(8,128)S(1)}, u32[]{:S(2)}, u32[]{:S(2)}) %collective-permute-start.2) | collective-permute-done | bytes 69664 | tf_op jit(solution)/shard_map/ppermute | solution.py:53
  17.5 0.7 collective-permute-start.4
  18.2 3.8 %collective-permute-done.4 = f32[144,128]{1,0:T(8,128)S(1)} collective-permute-done((f32[144,128]{1,0:T(8,128)S(1)}, f32[144,128]{1,0:T(8,128)S(1)}, u32[]{:S(2)}, u32[]{:S(2)}) %collective-permute-start.4) | collective-permute-done | bytes 73760 | tf_op jit(solution)/shard_map/ppermute | solution.py:53
  22.0 6.9 %collective-permute-start.7 = (f32[152,128]{1,0:T(8,128)S(1)}, f32[152,128]{1,0:T(8,128)S(1)}, u32[]{:S(2)}, u32[]{:S(2)}) collective-permute-start(f32[152,128]{1,0:T(8,128)S(1)} %pad_maximum_fusion), channel_id=1, source_target_pairs={{0,32},{8,40},{16,48},{24,56},{32,0},{40,8},{48,16},{56,24},{64,96... | collective-permute-start | bytes 233480 | tf_op jit(solution)/shard_map/ppermute | solution.py:53
  28.9 2.9 %collective-permute-start.5 = (f32[152,128]{1,0:T(8,128)S(1)}, f32[152,128]{1,0:T(8,128)S(1)}, u32[]{:S(2)}, u32[]{:S(2)}) collective-permute-start(f32[152,128]{1,0:T(8,128)S(1)} %pad_maximum_fusion), channel_id=1, source_target_pairs={{0,16},{8,24},{16,32},{24,40},{32,48},{40,56},{48,0},{56,8},{64,80... | collective-permute-start | bytes 233480 | tf_op jit(solution)/shard_map/ppermute | solution.py:53
  32.1 2.2 %collective-permute-done.6 = f32[152,128]{1,0:T(8,128)S(1)} collective-permute-done((f32[152,128]{1,0:T(8,128)S(1)}, f32[152,128]{1,0:T(8,128)S(1)}, u32[]{:S(2)}, u32[]{:S(2)}) %collective-permute-start.6) | collective-permute-done | bytes 77856 | tf_op jit(solution)/shard_map/ppermute | solution.py:53
  34.3 2.0 %collective-permute-done.5 = f32[152,128]{1,0:T(8,128)S(1)} collective-permute-done((f32[152,128]{1,0:T(8,128)S(1)}, f32[152,128]{1,0:T(8,128)S(1)}, u32[]{:S(2)}, u32[]{:S(2)}) %collective-permute-start.5) | collective-permute-done | bytes 77856 | tf_op jit(solution)/shard_map/ppermute | solution.py:53
  36.4 2.8 %collective-permute-start.10 = (f32[200,128]{1,0:T(8,128)S(1)}, f32[200,128]{1,0:T(8,128)S(1)}, u32[]{:S(2)}, u32[]{:S(2)}) collective-permute-start(f32[200,128]{1,0:T(8,128)S(1)} %constant_dynamic-update-slice_fusion.refs_0_), channel_id=1, source_target_pairs={{0,192},{8,200},{16,208},{24,216},{32,224},{40,232},{48,240},{56,2... | collective-permute-start | bytes 307208 | tf_op jit(solution)/shard_map/ppermute | solution.py:53
  39.2 0.9 %collective-permute-start.8 = (f32[200,128]{1,0:T(8,128)S(1)}, f32[200,128]{1,0:T(8,128)S(1)}, u32[]{:S(2)}, u32[]{:S(2)}) collective-permute-start(f32[200,128]{1,0:T(8,128)S(1)} %constant_dynamic-update-slice_fusion.refs_0_), channel_id=1, source_target_pairs={{0,64},{8,72},{16,80},{24,88},{32,96},{40,104},{48,112},{56,120},{... | collective-permute-start | bytes 307208 | tf_op jit(solution)/shard_map/ppermute | solution.py:53
  40.1 2.3 %collective-permute-done.10.refs_3_ = f32[200,128]{1,0:T(8,128)S(1)} collective-permute-done((f32[200,128]{1,0:T(8,128)S(1)}, f32[200,128]{1,0:T(8,128)S(1)}, u32[]{:S(2)}, u32[]{:S(2)}) %collective-permute-start.10) | collective-permute-done | bytes 102432 | tf_op jit(solution)/shard_map/ppermute | solution.py:53
  42.5 3.0 %collective-permute-done.9.refs_2_ = f32[200,128]{1,0:T(8,128)S(1)} collective-permute-done((f32[200,128]{1,0:T(8,128)S(1)}, f32[200,128]{1,0:T(8,128)S(1)}, u32[]{:S(2)}, u32[]{:S(2)}) %collective-permute-start.9) | collective-permute-done | bytes 102432 | tf_op jit(solution)/shard_map/ppermute | solution.py:53
  45.4 0.8 %collective-permute-done.8.refs_1_ = f32[200,128]{1,0:T(8,128)S(1)} collective-permute-done((f32[200,128]{1,0:T(8,128)S(1)}, f32[200,128]{1,0:T(8,128)S(1)}, u32[]{:S(2)}, u32[]{:S(2)}) %collective-permute-start.8) | collective-permute-done | bytes 102432 | tf_op jit(solution)/shard_map/ppermute | solution.py:53
  46.7 0.8 %collective-permute-done.12.refs_5_ = f32[200,128]{1,0:T(8,128)S(1)} collective-permute-done((f32[200,128]{1,0:T(8,128)S(1)}, f32[200,128]{1,0:T(8,128)S(1)}, u32[]{:S(2)}, u32[]{:S(2)}) %collective-permute-start.12) | collective-permute-done | bytes 102432 | tf_op jit(solution)/shard_map/ppermute | solution.py:53
  47.5 13.5 %shard_map.84 = f32[64,128]{1,0:T(8,128)S(1)} custom-call(f32[200,128]{1,0:T(8,128)S(1)} %constant_dynamic-update-slice_fusion.refs_0_, f32[200,128]{1,0:T(8,128)S(1)} %collective-permute-done.8.refs_1_, f32[200,128]{1,0:T(8,128)S(1)} %collective-permute-done.9.refs_2_, f32[200,128]{1,0:T(8,128)S(1)} %collective-permute-done.10.refs_3_, ...), custom_call_target="tpu_custom_call" | custom-call | tf_op jit(solution)/shard_map/pallas_call | solution.py:450
  61.0 3.0 %collective-permute-start.17 = (f32[64,128]{1,0:T(8,128)S(1)}, f32[64,128]{1,0:T(8,128)S(1)}, u32[]{:S(2)}, u32[]{:S(2)}) collective-permute-start(f32[64,128]{1,0:T(8,128)S(1)} %shard_map.84), channel_id=1, source_target_pairs={{0,6},{2,4},{4,2},{6,0},{1,7},{3,5},{5,3},{7,1},{8,14},{10,12},{12... | collective-permute-start | bytes 98312 | tf_op jit(solution)/shard_map/ppermute | solution.py:53
  64.0 0.8 %collective-permute-start.16 = (f32[64,128]{1,0:T(8,128)S(1)}, f32[64,128]{1,0:T(8,128)S(1)}, u32[]{:S(2)}, u32[]{:S(2)}) collective-permute-start(f32[64,128]{1,0:T(8,128)S(1)} %shard_map.84), channel_id=1, source_target_pairs={{0,4},{2,6},{4,0},{6,2},{1,5},{3,7},{5,1},{7,3},{8,12},{10,14},{12... | collective-permute-start | bytes 98312 | tf_op jit(solution)/shard_map/ppermute | solution.py:53
  65.2 1.0 %collective-permute-done.17 = f32[64,128]{1,0:T(8,128)S(1)} collective-permute-done((f32[64,128]{1,0:T(8,128)S(1)}, f32[64,128]{1,0:T(8,128)S(1)}, u32[]{:S(2)}, u32[]{:S(2)}) %collective-permute-start.17) | collective-permute-done | bytes 32800 | tf_op jit(solution)/shard_map/ppermute | solution.py:53
  66.2 3.2 %collective-permute-done.16 = f32[64,128]{1,0:T(8,128)S(1)} collective-permute-done((f32[64,128]{1,0:T(8,128)S(1)}, f32[64,128]{1,0:T(8,128)S(1)}, u32[]{:S(2)}, u32[]{:S(2)}) %collective-permute-start.16) | collective-permute-done | bytes 32800 | tf_op jit(solution)/shard_map/ppermute | solution.py:53
  (27 shorter events, 2.8 us)
Async XLA Ops:
  6.4 1.4 %collective-permute-start = (f32[64,512]{1,0:T(8,128)S(1)}, f32[64,512]{1,0:T(8,128)S(1)}, u32[]{:S(2)}, u32[]{:S(2)}) collective-permute-start(f32[64,512]{1,0:T(8,128)S(1)} %get-tuple-element.11.own_ref.refs_8_), channel_id=1, source_target_pairs={{0,1},{1,0},{2,3},{3,2},{4,5},{5,4},{6,7},{7,6},{8,9},{9,8},{10,11... | collective-permute-start | bytes 393224 | tf_op jit(solution)/shard_map/ppermute | solution.py:53
  8.6 5.9 %collective-permute-start.1 = (f32[136,128]{1,0:T(8,128)S(1)}, f32[136,128]{1,0:T(8,128)S(1)}, u32[]{:S(2)}, u32[]{:S(2)}) collective-permute-start(f32[136,128]{1,0:T(8,128)S(1)} %get-tuple-element.13), channel_id=1, source_target_pairs={{0,64},{8,72},{16,80},{24,88},{32,96},{40,104},{48,112},{56,120},{... | collective-permute-start | bytes 208904 | tf_op jit(solution)/shard_map/ppermute | solution.py:53
  10.3 6.6 %collective-permute-start.2 = (f32[136,128]{1,0:T(8,128)S(1)}, f32[136,128]{1,0:T(8,128)S(1)}, u32[]{:S(2)}, u32[]{:S(2)}) collective-permute-start(f32[136,128]{1,0:T(8,128)S(1)} %get-tuple-element.14), channel_id=1, source_target_pairs={{0,128},{8,136},{16,144},{24,152},{32,160},{40,168},{48,176},{56,1... | collective-permute-start | bytes 208904 | tf_op jit(solution)/shard_map/ppermute | solution.py:53
  13.2 4.3 %collective-permute-start.3 = (f32[136,128]{1,0:T(8,128)S(1)}, f32[136,128]{1,0:T(8,128)S(1)}, u32[]{:S(2)}, u32[]{:S(2)}) collective-permute-start(f32[136,128]{1,0:T(8,128)S(1)} %get-tuple-element.15), channel_id=1, source_target_pairs={{0,192},{8,200},{16,208},{24,216},{32,224},{40,232},{48,240},{56,2... | collective-permute-start | bytes 208904 | tf_op jit(solution)/shard_map/ppermute | solution.py:53
  17.5 4.4 %collective-permute-start.4 = (f32[144,128]{1,0:T(8,128)S(1)}, f32[144,128]{1,0:T(8,128)S(1)}, u32[]{:S(2)}, u32[]{:S(2)}) collective-permute-start(f32[144,128]{1,0:T(8,128)S(1)} %pad_maximum_fusion.1), channel_id=1, source_target_pairs={{0,8},{8,0},{16,24},{24,16},{32,40},{40,32},{48,56},{56,48},{64,72... | collective-permute-start | bytes 221192 | tf_op jit(solution)/shard_map/ppermute | solution.py:53
  22.0 10.1 %collective-permute-start.7 = (f32[152,128]{1,0:T(8,128)S(1)}, f32[152,128]{1,0:T(8,128)S(1)}, u32[]{:S(2)}, u32[]{:S(2)}) collective-permute-start(f32[152,128]{1,0:T(8,128)S(1)} %pad_maximum_fusion), channel_id=1, source_target_pairs={{0,32},{8,40},{16,48},{24,56},{32,0},{40,8},{48,16},{56,24},{64,96... | collective-permute-start | bytes 233480 | tf_op jit(solution)/shard_map/ppermute | solution.py:53
  28.9 5.4 %collective-permute-start.6 = (f32[152,128]{1,0:T(8,128)S(1)}, f32[152,128]{1,0:T(8,128)S(1)}, u32[]{:S(2)}, u32[]{:S(2)}) collective-permute-start(f32[152,128]{1,0:T(8,128)S(1)} %pad_maximum_fusion), channel_id=1, source_target_pairs={{0,48},{8,56},{16,0},{24,8},{32,16},{40,24},{48,32},{56,40},{64,11... | collective-permute-start | bytes 233480 | tf_op jit(solution)/shard_map/ppermute | solution.py:53
  28.9 7.3 %collective-permute-start.5 = (f32[152,128]{1,0:T(8,128)S(1)}, f32[152,128]{1,0:T(8,128)S(1)}, u32[]{:S(2)}, u32[]{:S(2)}) collective-permute-start(f32[152,128]{1,0:T(8,128)S(1)} %pad_maximum_fusion), channel_id=1, source_target_pairs={{0,16},{8,24},{16,32},{24,40},{32,48},{40,56},{48,0},{56,8},{64,80... | collective-permute-start | bytes 233480 | tf_op jit(solution)/shard_map/ppermute | solution.py:53
  36.4 6.1 %collective-permute-start.10 = (f32[200,128]{1,0:T(8,128)S(1)}, f32[200,128]{1,0:T(8,128)S(1)}, u32[]{:S(2)}, u32[]{:S(2)}) collective-permute-start(f32[200,128]{1,0:T(8,128)S(1)} %constant_dynamic-update-slice_fusion.refs_0_), channel_id=1, source_target_pairs={{0,192},{8,200},{16,208},{24,216},{32,224},{40,232},{48,240},{56,2... | collective-permute-start | bytes 307208 | tf_op jit(solution)/shard_map/ppermute | solution.py:53
  39.1 6.3 %collective-permute-start.9 = (f32[200,128]{1,0:T(8,128)S(1)}, f32[200,128]{1,0:T(8,128)S(1)}, u32[]{:S(2)}, u32[]{:S(2)}) collective-permute-start(f32[200,128]{1,0:T(8,128)S(1)} %constant_dynamic-update-slice_fusion.refs_0_), channel_id=1, source_target_pairs={{0,128},{8,136},{16,144},{24,152},{32,160},{40,168},{48,176},{56,1... | collective-permute-start | bytes 307208 | tf_op jit(solution)/shard_map/ppermute | solution.py:53
  39.2 7.0 %collective-permute-start.8 = (f32[200,128]{1,0:T(8,128)S(1)}, f32[200,128]{1,0:T(8,128)S(1)}, u32[]{:S(2)}, u32[]{:S(2)}) collective-permute-start(f32[200,128]{1,0:T(8,128)S(1)} %constant_dynamic-update-slice_fusion.refs_0_), channel_id=1, source_target_pairs={{0,64},{8,72},{16,80},{24,88},{32,96},{40,104},{48,112},{56,120},{... | collective-permute-start | bytes 307208 | tf_op jit(solution)/shard_map/ppermute | solution.py:53
  40.1 6.1 %collective-permute-start.11 = (f32[200,128]{1,0:T(8,128)S(1)}, f32[200,128]{1,0:T(8,128)S(1)}, u32[]{:S(2)}, u32[]{:S(2)}) collective-permute-start(f32[200,128]{1,0:T(8,128)S(1)} %constant_dynamic-update-slice_fusion.refs_0_), channel_id=1, source_target_pairs={{0,1},{1,0},{2,3},{3,2},{4,5},{5,4},{6,7},{7,6},{8,9},{9,8},{10,11... | collective-permute-start | bytes 307208 | tf_op jit(solution)/shard_map/ppermute | solution.py:53
  42.4 3.8 %collective-permute-start.14 = (f32[200,128]{1,0:T(8,128)S(1)}, f32[200,128]{1,0:T(8,128)S(1)}, u32[]{:S(2)}, u32[]{:S(2)}) collective-permute-start(f32[200,128]{1,0:T(8,128)S(1)} %collective-permute-done.10.refs_3_), channel_id=1, source_target_pairs={{0,1},{1,0},{2,3},{3,2},{4,5},{5,4},{6,7},{7,6},{8,9},{9,8},{10,11... | collective-permute-start | bytes 307208 | tf_op jit(solution)/shard_map/ppermute | solution.py:53
  45.4 1.3 %collective-permute-start.13 = (f32[200,128]{1,0:T(8,128)S(1)}, f32[200,128]{1,0:T(8,128)S(1)}, u32[]{:S(2)}, u32[]{:S(2)}) collective-permute-start(f32[200,128]{1,0:T(8,128)S(1)} %collective-permute-done.9.refs_2_), channel_id=1, source_target_pairs={{0,1},{1,0},{2,3},{3,2},{4,5},{5,4},{6,7},{7,6},{8,9},{9,8},{10,11... | collective-permute-start | bytes 307208 | tf_op jit(solution)/shard_map/ppermute | solution.py:53
  46.2 1.3 %collective-permute-start.12 = (f32[200,128]{1,0:T(8,128)S(1)}, f32[200,128]{1,0:T(8,128)S(1)}, u32[]{:S(2)}, u32[]{:S(2)}) collective-permute-start(f32[200,128]{1,0:T(8,128)S(1)} %collective-permute-done.8.refs_1_), channel_id=1, source_target_pairs={{0,1},{1,0},{2,3},{3,2},{4,5},{5,4},{6,7},{7,6},{8,9},{9,8},{10,11... | collective-permute-start | bytes 307208 | tf_op jit(solution)/shard_map/ppermute | solution.py:53
  61.0 5.2 %collective-permute-start.17 = (f32[64,128]{1,0:T(8,128)S(1)}, f32[64,128]{1,0:T(8,128)S(1)}, u32[]{:S(2)}, u32[]{:S(2)}) collective-permute-start(f32[64,128]{1,0:T(8,128)S(1)} %shard_map.84), channel_id=1, source_target_pairs={{0,6},{2,4},{4,2},{6,0},{1,7},{3,5},{5,3},{7,1},{8,14},{10,12},{12... | collective-permute-start | bytes 98312 | tf_op jit(solution)/shard_map/ppermute | solution.py:53
  64.0 5.4 %collective-permute-start.16 = (f32[64,128]{1,0:T(8,128)S(1)}, f32[64,128]{1,0:T(8,128)S(1)}, u32[]{:S(2)}, u32[]{:S(2)}) collective-permute-start(f32[64,128]{1,0:T(8,128)S(1)} %shard_map.84), channel_id=1, source_target_pairs={{0,4},{2,6},{4,0},{6,2},{1,5},{3,7},{5,1},{7,3},{8,12},{10,14},{12... | collective-permute-start | bytes 98312 | tf_op jit(solution)/shard_map/ppermute | solution.py:53
  64.8 4.6 %collective-permute-start.15 = (f32[64,128]{1,0:T(8,128)S(1)}, f32[64,128]{1,0:T(8,128)S(1)}, u32[]{:S(2)}, u32[]{:S(2)}) collective-permute-start(f32[64,128]{1,0:T(8,128)S(1)} %shard_map.84), channel_id=1, source_target_pairs={{0,2},{2,0},{4,6},{6,4},{1,3},{3,1},{5,7},{7,5},{8,10},{10,8},{12,... | collective-permute-start | bytes 98312 | tf_op jit(solution)/shard_map/ppermute | solution.py:53
